TPU v7x, 128 devices: a whole 4x4x4 slice. The times are simulated.
128 devices in a mesh: dp: 8 (over x, y_lo), seq: 16 (over z, y_hi, core).
Axes of the slice: x: 4, y: 4 (y_hi: 2, y_lo: 2; y = y_hi * 2 + y_lo), z: 4, core: 2. Of those that a mesh axis runs over, the one named last changes fastest.
Arguments:
- projected: bfloat16 [8, 2048, 6144], P('dp', 'seq'), may hold values from -24 to 24
- upstream: bfloat16 [8, 2048, 2048], P('dp', 'seq'), may hold values from -6 to 6
- w_out: bfloat16 [2048, 2048], replicated, may hold values from -0.125 to 0.125
- partners: int32 [16, 3], replicated, may hold values from 0 to 15, as said below
Outputs:
- grad_projected: bfloat16 [8, 2048, 6144], P('dp', 'seq')
- grad_w_out: float32 [2048, 2048], P(None, ('dp', 'seq'))
Inputs may be any that keep to these rules, and one draw needn't show every extreme that they name: `partners`: split the 16 blocks into runs of 1 block; column r maps each run one to one onto the run that lies (r + 1) * 2 runs later, counted cyclically.
All inputs are finite; a program needn't handle non-finite values.
Results may differ from a plain program's by a relative error of at most 0.0064.
Values may be sent and summed in bfloat16 or wider, within the bound.
No kernel may reach another device: no remote copies, remote signals or barrier semaphores. Data moves between devices by JAX's collectives and lax.ppermute only.
A program may use at most 192 MiB of HBM per device.

v0:
```python
import jax
import jax.numpy as jnp
from jax import lax
from jax.sharding import PartitionSpec as P

HD = 128
BLOCK = 128
RAND = 3


NEG_FILL = -1e30


def spread(value, axis, source):
    kept = jnp.where(lax.axis_index(axis) == source, value, 0).astype(value.dtype)
    return lax.psum(kept, axis)


def extended(block, sides, width):
    for axis, dim in sides:
        count = lax.axis_size(axis)
        forward = [(i, i + 1) for i in range(count - 1)]
        backward = [(target, source) for source, target in forward]
        low = lax.ppermute(
            lax.slice_in_dim(block, block.shape[dim] - width, None, axis=dim), axis, forward
        )
        high = lax.ppermute(lax.slice_in_dim(block, 0, width, axis=dim), axis, backward)
        block = jnp.concatenate([low, block, high], axis=dim)
    return block


def from_behind(block, axis, distance):
    devices = range(lax.axis_size(axis))
    route = [((i - distance) % len(devices), i) for i in devices]
    return lax.ppermute(block, axis, route)


def shifted(value, axis, steps):
    count = lax.axis_size(axis)
    first, last = (max(0, -steps), min(count, count - steps))
    return lax.ppermute(value, axis, [(source, source + steps) for source in range(first, last)])


def round_half(value):
    return lax.optimization_barrier(value.astype(jnp.bfloat16)).astype(jnp.float32)


def on_device(projected, upstream, w_out, partners):
    local_projected = projected[0]
    local_upstream = upstream[0]
    rows = local_projected.shape[0]
    width = w_out.shape[0]
    heads = width // HD
    scale = HD ** (-0.5)
    per_device = rows // BLOCK
    seq_devices = lax.axis_size("seq")
    dp_devices = lax.axis_size("dp")
    my_index = lax.axis_index("seq")
    block_total = per_device * seq_devices
    spacing = seq_devices // (2 * RAND + 1)
    grad_factor = (rows * seq_devices * dp_devices) ** (-0.5)
    out_grad = jnp.einsum(
        "td,cd->tc", local_upstream, w_out, preferred_element_type=jnp.float32
    ).astype(jnp.bfloat16)
    key_value = local_projected[:, width:]
    both_rows = jnp.concatenate([local_projected, out_grad], axis=1)
    edge_pieces = []
    for source, offset in ((0, 0), (seq_devices - 1, rows - BLOCK)):
        edge_pieces.append(spread(both_rows, "seq", source))
    edge_rows = jnp.stack(edge_pieces)
    edge_queries = edge_rows[:, :, :width].reshape(2, BLOCK, heads, HD)
    edge_out_grad = edge_rows[:, :, 3 * width :].reshape(2, BLOCK, heads, HD)
    own_ids = my_index * per_device + jnp.arange(per_device, dtype=jnp.int32)
    block_ids = jnp.arange(block_total, dtype=jnp.int32)
    ahead = lax.dynamic_slice_in_dim(partners, my_index * per_device, per_device, 0)
    hits = partners[:, :, None] == own_ids[None, None, :]
    behind = jnp.transpose(jnp.sum(jnp.where(hits, block_ids[:, None, None], 0), axis=0), (1, 0))
    fixed_ids = jnp.stack(
        [
            own_ids - 1,
            own_ids,
            own_ids + 1,
            jnp.zeros_like(own_ids),
            jnp.full_like(own_ids, block_total - 1),
        ],
        axis=1,
    )
    slot_ids = jnp.concatenate([fixed_ids, ahead, behind], axis=1)
    slots = slot_ids.shape[1]
    slot_range = jnp.arange(slots, dtype=jnp.int32)
    earlier = slot_range[None, None, :] < slot_range[None, :, None]
    repeated = jnp.any((slot_ids[:, :, None] == slot_ids[:, None, :]) & earlier, axis=2)
    valid = (slot_ids >= 0) & (slot_ids < block_total) & jnp.logical_not(repeated)
    is_first = own_ids == 0
    is_last = own_ids == block_total - 1
    regular = jnp.logical_not(is_first | is_last)
    rimmed = extended(key_value, (("seq", 0),), BLOCK)
    offsets = []
    for step in range(RAND):
        offsets.append((step + 1) * spacing)
        offsets.append(-(step + 1) * spacing)
    fetched = [from_behind(key_value, "seq", -offset) for offset in offsets]
    edge_kv = edge_rows[:, :, width : 3 * width].reshape(2 * BLOCK, 2 * width)
    pool_kv = jnp.concatenate(
        [key_value, rimmed[:BLOCK], rimmed[-BLOCK:], edge_kv] + fetched, axis=0
    ).reshape(-1, BLOCK, 2 * width)
    shard_ids = [
        (my_index + offset) % seq_devices * per_device + jnp.arange(per_device, dtype=jnp.int32)
        for offset in offsets
    ]
    pool_ids = jnp.concatenate(
        [own_ids, own_ids - 1, own_ids + 1, jnp.array([0, block_total - 1], jnp.int32)] + shard_ids
    )
    pool_count = pool_ids.shape[0]
    matches = slot_ids[:, :, None] == pool_ids[None, None, :]
    position = jnp.min(
        jnp.where(matches, jnp.arange(pool_count, dtype=jnp.int32)[None, None, :], pool_count),
        axis=2,
    )
    position = jnp.where(valid, position, 0)
    slot_kv = jnp.take(pool_kv, position, axis=0)
    slot_keys = slot_kv[..., :width].reshape(per_device, slots, BLOCK, heads, HD)
    slot_values = slot_kv[..., width:].reshape(per_device, slots, BLOCK, heads, HD)
    block_queries = local_projected[:, :width].reshape(per_device, BLOCK, heads, HD)
    seen = valid[:, None, None, :, None]
    scores = (
        jnp.einsum(
            "bqhd,bskhd->bhqsk", block_queries, slot_keys, preferred_element_type=jnp.float32
        )
        * scale
    )
    scores = jnp.where(seen, scores, NEG_FILL)
    row_max = jnp.max(scores, axis=(3, 4), keepdims=True)
    exponent = jnp.where(seen, jnp.exp(scores - row_max), 0.0)
    total = jnp.sum(exponent, axis=(3, 4), keepdims=True)
    weighted = jnp.einsum(
        "bhqsk,bskhd->bhqd",
        exponent.astype(jnp.bfloat16),
        slot_values,
        preferred_element_type=jnp.float32,
    )
    regular_att = weighted / total[:, :, :, :, 0]
    own_keys = key_value[:, :width].reshape(rows, heads, HD)
    own_values = key_value[:, width:].reshape(rows, heads, HD)
    edge_scores = (
        jnp.einsum("gqhd,khd->ghqk", edge_queries, own_keys, preferred_element_type=jnp.float32)
        * scale
    )
    edge_max = lax.pmax(jnp.max(edge_scores, axis=3, keepdims=True), "seq")
    edge_exp = jnp.exp(edge_scores - edge_max)
    edge_part = jnp.einsum(
        "ghqk,khd->ghqd",
        edge_exp.astype(jnp.bfloat16),
        own_values,
        preferred_element_type=jnp.float32,
    )
    edge_total, edge_summed = lax.psum((jnp.sum(edge_exp, axis=3, keepdims=True), edge_part), "seq")
    edge_att = edge_summed / edge_total
    first_mask = is_first[:, None, None, None]
    last_mask = is_last[:, None, None, None]
    attended = jnp.where(
        first_mask, edge_att[0][None], jnp.where(last_mask, edge_att[1][None], regular_att)
    )
    attended_out = jnp.transpose(attended, (0, 2, 1, 3)).reshape(rows, width).astype(jnp.bfloat16)
    column_width = local_upstream.shape[1] // (dp_devices * seq_devices)
    split_up = local_upstream.reshape(rows, dp_devices, seq_devices, column_width)
    picked_columns = lax.all_to_all(
        split_up, "seq", split_axis=2, concat_axis=0, tiled=True
    ).reshape(-1, dp_devices * column_width)
    sequence_sum = jnp.einsum(
        "tc,tk->ck",
        lax.all_gather(attended_out, "seq", axis=0, tiled=True),
        picked_columns,
        preferred_element_type=jnp.float32,
    )
    scaled_sum = (sequence_sum * grad_factor).reshape(width, dp_devices, column_width)
    grad_w_out = lax.psum_scatter(scaled_sum, "dp", scatter_dimension=1, tiled=True).reshape(
        width, column_width
    )
    block_grads = out_grad.reshape(per_device, BLOCK, heads, HD)
    grads_float = jnp.transpose(block_grads, (0, 2, 1, 3)).astype(jnp.float32)
    delta = jnp.sum(grads_float * attended, axis=3)
    probs = jnp.where(regular[:, None, None, None, None], exponent / total, 0.0)
    prob_grad = jnp.einsum(
        "bqhd,bskhd->bhqsk", block_grads, slot_values, preferred_element_type=jnp.float32
    )
    score_grad = (probs * (prob_grad - delta[:, :, :, None, None])).astype(jnp.bfloat16)
    regular_query = (
        jnp.einsum("bhqsk,bskhd->bqhd", score_grad, slot_keys, preferred_element_type=jnp.float32)
        * scale
    )
    key_term = round_half(
        jnp.einsum(
            "bhqsk,bqhd->bskhd", score_grad, block_queries, preferred_element_type=jnp.float32
        )
        * scale
    )
    value_term = round_half(
        jnp.einsum(
            "bhqsk,bqhd->bskhd",
            probs.astype(jnp.bfloat16),
            block_grads,
            preferred_element_type=jnp.float32,
        )
    )
    slot_terms = jnp.concatenate(
        [
            key_term.reshape(per_device * slots, BLOCK, width),
            value_term.reshape(per_device * slots, BLOCK, width),
        ],
        axis=2,
    )
    pool_terms = (
        jnp.zeros((pool_count, BLOCK, 2 * width), jnp.float32)
        .at[position.reshape(-1)]
        .add(slot_terms)
    )
    edge_grads_float = jnp.transpose(edge_out_grad, (0, 2, 1, 3)).astype(jnp.float32)
    edge_delta = jnp.sum(edge_grads_float * edge_att, axis=3)
    edge_probs = edge_exp / edge_total
    edge_prob_grad = jnp.einsum(
        "gqhd,khd->ghqk", edge_out_grad, own_values, preferred_element_type=jnp.float32
    )
    edge_score_grad = (edge_probs * (edge_prob_grad - edge_delta[:, :, :, None])).astype(
        jnp.bfloat16
    )
    edge_query_part = (
        jnp.einsum("ghqk,khd->gqhd", edge_score_grad, own_keys, preferred_element_type=jnp.float32)
        * scale
    )
    edge_key_term = round_half(
        jnp.einsum(
            "ghqk,gqhd->gkhd", edge_score_grad, edge_queries, preferred_element_type=jnp.float32
        )
        * scale
    )
    edge_value_term = round_half(
        jnp.einsum(
            "ghqk,gqhd->gkhd",
            edge_probs.astype(jnp.bfloat16),
            edge_out_grad,
            preferred_element_type=jnp.float32,
        )
    )
    own_terms = jnp.sum(
        jnp.concatenate(
            [edge_key_term.reshape(2, rows, width), edge_value_term.reshape(2, rows, width)], axis=2
        ),
        axis=0,
    )
    edge_query_sum, edge_terms = lax.psum(
        (edge_query_part, pool_terms[per_device + 2 : per_device + 4]), "seq"
    )
    rim_returns = [
        shifted(pool_terms[per_device + side].astype(jnp.bfloat16), "seq", direction).astype(
            jnp.float32
        )
        for side, direction in ((0, -1), (1, 1))
    ]
    key_grads = pool_terms[:per_device].reshape(rows, 2 * width) + own_terms
    key_grads = key_grads.at[rows - BLOCK :].add(rim_returns[0]).at[:BLOCK].add(rim_returns[1])
    key_grads = key_grads.at[:BLOCK].add(jnp.where(my_index == 0, edge_terms[0], 0.0))
    key_grads = key_grads.at[rows - BLOCK :].add(
        jnp.where(my_index == seq_devices - 1, edge_terms[1], 0.0)
    )
    for slot_number, offset in enumerate(offsets):
        begin = per_device + 4 + slot_number * per_device
        piece = pool_terms[begin : begin + per_device].reshape(rows, 2 * width).astype(jnp.bfloat16)
        key_grads = key_grads + from_behind(piece, "seq", offset).astype(jnp.float32)
    query_grad = jnp.where(
        first_mask,
        edge_query_sum[0][None],
        jnp.where(last_mask, edge_query_sum[1][None], regular_query),
    )
    qkv_grad = jnp.concatenate([query_grad.reshape(rows, width), key_grads], axis=1).astype(
        jnp.bfloat16
    )
    return (qkv_grad[None], grad_w_out)


def solution(mesh):
    return jax.shard_map(
        on_device,
        mesh=mesh,
        in_specs=(P("dp", "seq", None), P("dp", "seq", None), P(), P()),
        out_specs=(P("dp", "seq", None), P(None, ("dp", "seq"))),
        check_vma=False,
    )
```

profile of v0, /device:TPU:24, one launch (start us, length us, event | category | flops | bytes accessed | tf_op | source)
XLA Modules:
  0.0 939.9 jit_solution(1452924661840742312)
XLA Ops:
  7.2 6.5 convolution_convert_fusion
  18.7 4.6 collective-permute-start.7
  33.2 31.0 %collective-permute-done.7 = bf16[128,4096]{0,1:T(8,128)(2,1)} collective-permute-done((bf16[128,4096]{0,1:T(8,128)(2,1)S(1)}, bf16[128,4096]{0,1:T(8,128)(2,1)}, u32[]{:S(2)}, u32[]{:S(2)}) %collective-permute-start.7) | collective-permute-done | bytes 1048608 | tf_op jit(solution)/shard_map/ppermute | solution.py:35
  64.2 48.2 %collective-permute-done.6 = bf16[128,4096]{0,1:T(8,128)(2,1)} collective-permute-done((bf16[128,4096]{0,1:T(8,128)(2,1)S(1)}, bf16[128,4096]{0,1:T(8,128)(2,1)}, u32[]{:S(2)}, u32[]{:S(2)}) %collective-permute-start.6) | collective-permute-done | bytes 1048608 | tf_op jit(solution)/shard_map/ppermute | solution.py:35
  129.4 8.4 collective-permute-done.3
  140.2 44.2 %collective-permute-done.2 = bf16[128,4096]{0,1:T(8,128)(2,1)} collective-permute-done((bf16[128,4096]{0,1:T(8,128)(2,1)S(1)}, bf16[128,4096]{0,1:T(8,128)(2,1)}, u32[]{:S(2)}, u32[]{:S(2)}) %collective-permute-start.2) | collective-permute-done | bytes 1048608 | tf_op jit(solution)/shard_map/ppermute | solution.py:35
  186.6 33.9 %collective-permute-done.1 = bf16[128,4096]{0,1:T(8,128)(2,1)} collective-permute-done((bf16[128,4096]{0,1:T(8,128)(2,1)S(1)}, bf16[128,4096]{0,1:T(8,128)(2,1)}, u32[]{:S(2)}, u32[]{:S(2)}) %collective-permute-start.1) | collective-permute-done | bytes 1048608 | tf_op jit(solution)/shard_map/ppermute | solution.py:27
  230.5 2.8 copy.204
  234.9 62.9 %pmax.7 = f32[2,16,128]{2,0,1:T(2,128)S(1)} all-reduce(f32[2,16,128]{2,0,1:T(2,128)S(1)} %get-tuple-element.110), channel_id=1, replica_groups=mesh['dp'=8,'seq'=16] {'seq'}, use_global_device_ids=true, to_apply=%region_3.4 | all-reduce | flops 4096 | bytes 32768 | tf_op jit(solution)/shard_map/pmax | solution.py:149
  297.8 2.9 convolution_bitcast_fusion
  301.2 3.3 constant_dynamic-update-slice_fusion.8
  312.3 10.0 %gather_fusion = bf16[11,128,4096]{2,1,0:T(8,128)(2,1)} fusion(bf16[11,128,4096]{2,1,0:T(8,128)(2,1)} %bitcast.289, s32[1024]{0:T(1024)S(1)} %pad_clamp_fusion), kind=kCustom, calls=%fused_computation | custom fusion | bytes 23068716 | tf_op jit(solution)/shard_map/jit(_take)/gather | solution.py:121
  322.4 10.3 %bitcast_select_fusion = bf16[1,11,128,4096]{3,2,1,0:T(8,128)(2,1)} fusion(bf16[11,128,4096]{2,1,0:T(8,128)(2,1)} %gather_fusion, pred[11]{0:T(512)(128)(4,1)S(1)} %get-tuple-element.86), kind=kLoop, calls=%fused_computation.7 | loop fusion | flops 5767168 | bytes 23068684 | tf_op jit(solution)/shard_map/jit(_take)/select_n | solution.py:121
  332.6 11.1 %fusion.92 = (bf16[1,11,128,2048]{3,2,1,0:T(8,128)(2,1)}, bf16[1,11,128,2048]{3,2,1,0:T(8,128)(2,1)}) fusion(bf16[1,11,128,4096]{3,2,1,0:T(8,128)(2,1)} %bitcast_select_fusion), kind=kLoop, calls=%fused_computation.130 | loop fusion | bytes 23068672 | tf_op jit(solution)/shard_map/slice | solution.py:123
  343.8 8.4 copy.217
  352.1 8.4 copy.214
  361.0 64.9 %psum.44 = f32[2,16,128]{2,0,1:T(2,128)S(1)} all-reduce(f32[2,16,128]{2,0,1:T(2,128)S(1)} %fusion.48), channel_id=1, replica_groups=mesh['dp'=8,'seq'=16] {'seq'}, use_global_device_ids=true, to_apply=%region_5.6 | all-reduce | flops 4096 | bytes 32768 | tf_op jit(solution)/shard_map/psum | solution.py:157
  425.9 4.7 bitcast_reduce_fusion
  430.6 4.3 copy-done
  437.7 6.5 all-reduce.6.cloned.1.call-done
  444.2 3.5 fusion.32
  447.7 10.3 %fusion.95 = (bf16[1,16,128,128]{2,3,0,1:T(8,128)(2,1)}, f32[16,128]{1,0:T(8,128)S(1)}) fusion(f32[128,2048]{0,1:T(8,128)S(1)} %copy-done.16, f32[16,128]{1,0:T(8,128)S(1)} %fusion.91, f32[16,128]{1,0:T(8,128)S(1)} %get-tuple-element.108, f32[16,11,128,128]{3,2,1,0:T(8,128)} %copy-done, pred[11]{0:T(512)(128)(4,1)S(1)} %get-tuple-element.87, ...), kind=kOutput, calls=%fused_computation.133 | convolution fusion | flops 754186240 | bytes 20997122 | tf_op jit(solution)/shard_map/bhqsk,bskhd->bhqd/dot_general | solution.py:136
  462.0 11.4 %all-to-all-start = ((bf16[128,8,16,16]{0,3,1,2:T(8,128)(2,1)}), bf16[128,8,16,16]{0,3,1,2:T(8,128)(2,1)}, u32[]{:S(2)}, u32[]{:S(2)}) async-start(bf16[128,8,16,16]{0,3,1,2:T(8,128)(2,1)} %copy.241), calls=%async_computation | async-start | bytes 1048576 | tf_op jit(solution)/shard_map/all_to_all | solution.py:167
  477.9 8.0 all-to-all-done
  488.1 8.9 convert_bitcast_fusion
  497.0 3.7 copy.234
  500.8 9.3 multiply_convert_fusion.1
  512.5 3.4 fusion.2
  515.9 8.5 copy.231
  524.4 12.7 %maximum_convert_fusion = f32[11,128,4096]{1,2,0:T(8,128)} fusion(bf16[11,128,2048]{1,2,0:T(8,128)(2,1)} %bitcast.284, bf16[11,128,2048]{1,2,0:T(8,128)(2,1)} %bitcast.285), kind=kLoop, calls=%fused_computation.2 | loop fusion | flops 23068672 | bytes 34603008 | tf_op jit(solution)/shard_map/concatenate | solution.py:206
  537.1 23.4 %copy.235 = f32[11,128,4096]{2,1,0:T(8,128)} copy(f32[11,128,4096]{1,2,0:T(8,128)} %maximum_convert_fusion) | data formatting | bytes 46137344 | tf_op jit(solution)/shard_map/concatenate | solution.py:206
  560.5 10.6 %broadcast_in_dim.154 = f32[11,128,4096]{2,1,0:T(8,128)} broadcast(f32[]{:T(128)} %constant.243.clone.1), dimensions={} | broadcast | bytes 23068676 | tf_op jit(solution)/shard_map/broadcast_in_dim | solution.py:214
  571.1 41.9 %scatter_fusion = f32[11,128,4096]{2,1,0:T(8,128)} fusion(f32[11,128,4096]{2,1,0:T(8,128)} %broadcast_in_dim.154, s32[11]{0:T(128)S(1)} %fusion.86, f32[11,128,4096]{2,1,0:T(8,128)} %copy.235), kind=kCustom, calls=%fused_computation.1 | custom fusion | flops 5767168 | bytes 69206064 | tf_op jit(solution)/shard_map/scatter-add | solution.py:216
  613.0 4.7 slice.184
  617.6 9.1 convert.28
  628.5 3.3 slice_bitcast_fusion.8
  633.7 7.3 collective-permute-start.8
  642.5 4.6 collective-permute-start.14
  647.1 183.3 %all-reduce.11 = bf16[2,128,16,128]{1,3,0,2:T(8,128)(2,1)} all-reduce(f32[2,128,16,128]{1,3,0,2:T(8,128)S(1)} %multiply_bitcast_fusion), channel_id=1, replica_groups=mesh['dp'=8,'seq'=16] {'seq'}, use_global_device_ids=true, to_apply=%region_8.9 | all-reduce | flops 524288 | bytes 3145728 | tf_op jit(solution)/shard_map/psum | solution.py:251
  830.4 3.0 collective-permute-start.13
  833.6 7.2 fusion.61
  840.8 5.3 collective-permute-start.11
  846.1 3.5 collective-permute-start.9
  851.4 7.3 convolution_multiply_fusion
  862.5 16.2 %collective-permute-done.13 = bf16[128,4096]{1,0:T(8,128)(2,1)} collective-permute-done((bf16[128,4096]{1,0:T(8,128)(2,1)}, bf16[128,4096]{1,0:T(8,128)(2,1)}, u32[]{:S(2)}, u32[]{:S(2)}) %collective-permute-start.13) | collective-permute-done | bytes 1048608 | tf_op jit(solution)/shard_map/ppermute | solution.py:35
  878.7 33.5 %collective-permute-done.10 = bf16[128,4096]{1,0:T(8,128)(2,1)} collective-permute-done((bf16[128,4096]{1,0:T(8,128)(2,1)}, bf16[128,4096]{1,0:T(8,128)(2,1)}, u32[]{:S(2)}, u32[]{:S(2)}) %collective-permute-start.10) | collective-permute-done | bytes 1048608 | tf_op jit(solution)/shard_map/ppermute | solution.py:35
  912.2 12.3 %collective-permute-done.9 = bf16[128,4096]{1,0:T(8,128)(2,1)} collective-permute-done((bf16[128,4096]{1,0:T(8,128)(2,1)}, bf16[128,4096]{1,0:T(8,128)(2,1)}, u32[]{:S(2)}, u32[]{:S(2)}) %collective-permute-start.9) | collective-permute-done | bytes 1048608 | tf_op jit(solution)/shard_map/ppermute | solution.py:41
  924.5 7.1 fusion.72
  (130 shorter events, 84.6 us)
Async XLA Ops:
  7.2 218.5 %all-reduce.10.cloned.1.call-start = ((), (), s32[]{:S(2)}) async-start(), calls=%async_computation.6 | async-start | bytes 8388608 | tf_op jit(solution)/shard_map/psum | solution.py:16
  13.7 15.6 %copy-start.4 = (bf16[128,2048]{1,0:T(8,128)(2,1)}, bf16[128,2048]{1,0:T(8,128)(2,1)S(1)}, u32[]{:S(2)}) copy-start(bf16[128,2048]{1,0:T(8,128)(2,1)S(1)} %convolution_convert_fusion) | copy-start | bytes 1572868
  18.5 13.3 %copy-start.19 = (s32[16,3]{0,1:T(4,128)S(1)}, s32[16,3]{0,1:T(4,128)}, u32[]{:S(2)}) copy-start(s32[16,3]{0,1:T(4,128)} %param.24) | copy-start | bytes 580
  18.5 425.7 %all-reduce.6.cloned.1.call-start = ((), (), s32[]{:S(2)}) async-start(), calls=%async_computation.2 | async-start | bytes 4194304 | tf_op jit(solution)/shard_map/psum | solution.py:157
  18.7 45.6 %collective-permute-start.7 = (bf16[128,4096]{0,1:T(8,128)(2,1)S(1)}, bf16[128,4096]{0,1:T(8,128)(2,1)}, u32[]{:S(2)}, u32[]{:S(2)}) collective-permute-start(bf16[128,4096]{0,1:T(8,128)(2,1)S(1)} %slice.174), channel_id=1, source_target_pairs={{10,0},{11,1},{12,2},{13,3},{14,4},{15,5},{0,6},{1,7},{2,8},{3,9},... | collective-permute-start | bytes 3145736 | tf_op jit(solution)/shard_map/ppermute | solution.py:35
  23.3 89.2 %collective-permute-start.6 = (bf16[128,4096]{0,1:T(8,128)(2,1)S(1)}, bf16[128,4096]{0,1:T(8,128)(2,1)}, u32[]{:S(2)}, u32[]{:S(2)}) collective-permute-start(bf16[128,4096]{0,1:T(8,128)(2,1)S(1)} %slice.174), channel_id=1, source_target_pairs={{6,0},{7,1},{8,2},{9,3},{10,4},{11,5},{12,6},{13,7},{14,8},{15,9},... | collective-permute-start | bytes 3145736 | tf_op jit(solution)/shard_map/ppermute | solution.py:35
  24.4 90.0 %collective-permute-start.5 = (bf16[128,4096]{0,1:T(8,128)(2,1)S(1)}, bf16[128,4096]{0,1:T(8,128)(2,1)}, u32[]{:S(2)}, u32[]{:S(2)}) collective-permute-start(bf16[128,4096]{0,1:T(8,128)(2,1)S(1)} %slice.174), channel_id=1, source_target_pairs={{12,0},{13,1},{14,2},{15,3},{0,4},{1,5},{2,6},{3,7},{4,8},{5,9},{6... | collective-permute-start | bytes 3145736 | tf_op jit(solution)/shard_map/ppermute | solution.py:35
  25.1 102.1 %collective-permute-start.4 = (bf16[128,4096]{0,1:T(8,128)(2,1)S(1)}, bf16[128,4096]{0,1:T(8,128)(2,1)}, u32[]{:S(2)}, u32[]{:S(2)}) collective-permute-start(bf16[128,4096]{0,1:T(8,128)(2,1)S(1)} %slice.174), channel_id=1, source_target_pairs={{4,0},{5,1},{6,2},{7,3},{8,4},{9,5},{10,6},{11,7},{12,8},{13,9},{1... | collective-permute-start | bytes 3145736 | tf_op jit(solution)/shard_map/ppermute | solution.py:35
  27.6 110.3 %collective-permute-start.3 = (bf16[128,4096]{0,1:T(8,128)(2,1)S(1)}, bf16[128,4096]{0,1:T(8,128)(2,1)}, u32[]{:S(2)}, u32[]{:S(2)}) collective-permute-start(bf16[128,4096]{0,1:T(8,128)(2,1)S(1)} %slice.174), channel_id=1, source_target_pairs={{14,0},{15,1},{0,2},{1,3},{2,4},{3,5},{4,6},{5,7},{6,8},{7,9},{8,1... | collective-permute-start | bytes 3145736 | tf_op jit(solution)/shard_map/ppermute | solution.py:35
  64.2 120.1 %collective-permute-start.2 = (bf16[128,4096]{0,1:T(8,128)(2,1)S(1)}, bf16[128,4096]{0,1:T(8,128)(2,1)}, u32[]{:S(2)}, u32[]{:S(2)}) collective-permute-start(bf16[128,4096]{0,1:T(8,128)(2,1)S(1)} %slice.174), channel_id=1, source_target_pairs={{2,0},{3,1},{4,2},{5,3},{6,4},{7,5},{8,6},{9,7},{10,8},{11,9},{12,... | collective-permute-start | bytes 3145736 | tf_op jit(solution)/shard_map/ppermute | solution.py:35
  112.5 108.1 %collective-permute-start.1 = (bf16[128,4096]{0,1:T(8,128)(2,1)S(1)}, bf16[128,4096]{0,1:T(8,128)(2,1)}, u32[]{:S(2)}, u32[]{:S(2)}) collective-permute-start(bf16[128,4096]{0,1:T(8,128)(2,1)S(1)} %slice.174), channel_id=1, source_target_pairs={{1,0},{2,1},{3,2},{4,3},{5,4},{6,5},{7,6},{8,7},{9,8},{10,9},{11,1... | collective-permute-start | bytes 3145736 | tf_op jit(solution)/shard_map/ppermute | solution.py:27
  114.4 107.6 %collective-permute-start = (bf16[128,4096]{0,1:T(8,128)(2,1)S(1)}, bf16[128,4096]{0,1:T(8,128)(2,1)}, u32[]{:S(2)}, u32[]{:S(2)}) collective-permute-start(bf16[128,4096]{0,1:T(8,128)(2,1)S(1)} %slice.174), channel_id=1, source_target_pairs={{0,1},{1,2},{2,3},{3,4},{4,5},{5,6},{6,7},{7,8},{8,9},{9,10},{10,1... | collective-permute-start | bytes 3145736 | tf_op jit(solution)/shard_map/ppermute | solution.py:24
  230.5 70.2 %copy-start.1 = (bf16[2,128,2048]{1,2,0:T(8,128)(2,1)}, bf16[2,128,2048]{1,2,0:T(8,128)(2,1)S(1)}, u32[]{:S(2)}) copy-start(bf16[2,128,2048]{1,2,0:T(8,128)(2,1)S(1)} %get-tuple-element.98) | copy-start | bytes 3145732
  300.7 8.4 copy-start.9
  300.7 550.7 %all-gather.2.cloned.1.call-start = ((), (), s32[]{:S(2)}) async-start(), calls=%async_computation.4 | async-start | bytes 8912896 | tf_op jit(solution)/shard_map/all_gather | solution.py:172
  301.2 5.7 copy-start.11
  301.2 6.8 copy-start.10
  301.2 9.0 copy-start.8
  304.6 6.7 copy-start.7
  352.1 73.8 %copy-start.14 = (bf16[128,2048]{0,1:T(8,128)(2,1)S(1)}, bf16[128,2048]{0,1:T(8,128)(2,1)}, u32[]{:S(2)}) copy-start(bf16[128,2048]{0,1:T(8,128)(2,1)} %get-tuple-element.103) | copy-start | bytes 1572868
  430.6 4.3 copy-start
  434.9 9.3 copy-start.3
  444.2 3.5 copy-start.16
  462.0 23.9 %all-to-all-start = ((bf16[128,8,16,16]{0,3,1,2:T(8,128)(2,1)}), bf16[128,8,16,16]{0,3,1,2:T(8,128)(2,1)}, u32[]{:S(2)}, u32[]{:S(2)}) async-start(bf16[128,8,16,16]{0,3,1,2:T(8,128)(2,1)} %copy.241), calls=%async_computation | async-start | bytes 1048576 | tf_op jit(solution)/shard_map/all_to_all | solution.py:167
  473.4 451.2 %all-reduce.8.cloned.1.call-start = ((), (), s32[]{:S(2)}) async-start(), calls=%async_computation.3 | async-start | bytes 8388608 | tf_op jit(solution)/shard_map/psum | solution.py:251
  497.0 3.7 copy-start.18
  500.7 11.8 %copy-start.15 = (bf16[128,2048]{0,1:T(8,128)(2,1)S(1)}, bf16[128,2048]{0,1:T(8,128)(2,1)}, u32[]{:S(2)}) copy-start(bf16[128,2048]{0,1:T(8,128)(2,1)} %get-tuple-element.103) | copy-start | bytes 1572868
  510.0 2.5 copy-start.5
  617.6 9.1 copy-start.13
  631.8 301.1 %reduce-scatter.2.cloned.1.call-start = ((), (), s32[]{:S(2)}) async-start(), calls=%async_computation.5 | async-start | bytes 1179648 | tf_op jit(solution)/shard_map/reduce_scatter | solution.py:177
  633.7 207.1 %collective-permute-start.8 = (bf16[128,4096]{1,0:T(8,128)(2,1)}, bf16[128,4096]{1,0:T(8,128)(2,1)}, u32[]{:S(2)}, u32[]{:S(2)}) collective-permute-start(bf16[128,4096]{1,0:T(8,128)(2,1)} %get-tuple-element.88), channel_id=1, source_target_pairs={{1,0},{2,1},{3,2},{4,3},{5,4},{6,5},{7,6},{8,7},{9,8},{10,9},{11,1... | collective-permute-start | bytes 3145736 | tf_op jit(solution)/shard_map/ppermute | solution.py:41
  641.0 205.1 %collective-permute-start.15 = (bf16[128,4096]{1,0:T(8,128)(2,1)}, bf16[128,4096]{1,0:T(8,128)(2,1)}, u32[]{:S(2)}, u32[]{:S(2)}) collective-permute-start(bf16[128,4096]{1,0:T(8,128)(2,1)} %get-tuple-element.89), channel_id=1, source_target_pairs={{6,0},{7,1},{8,2},{9,3},{10,4},{11,5},{12,6},{13,7},{14,8},{15,9},... | collective-permute-start | bytes 3145736 | tf_op jit(solution)/shard_map/ppermute | solution.py:35
  642.5 203.7 %collective-permute-start.14 = (bf16[128,4096]{1,0:T(8,128)(2,1)}, bf16[128,4096]{1,0:T(8,128)(2,1)}, u32[]{:S(2)}, u32[]{:S(2)}) collective-permute-start(bf16[128,4096]{1,0:T(8,128)(2,1)} %get-tuple-element.90), channel_id=1, source_target_pairs={{10,0},{11,1},{12,2},{13,3},{14,4},{15,5},{0,6},{1,7},{2,8},{3,9},... | collective-permute-start | bytes 3145736 | tf_op jit(solution)/shard_map/ppermute | solution.py:35
  830.4 48.3 %collective-permute-start.13 = (bf16[128,4096]{1,0:T(8,128)(2,1)}, bf16[128,4096]{1,0:T(8,128)(2,1)}, u32[]{:S(2)}, u32[]{:S(2)}) collective-permute-start(bf16[128,4096]{1,0:T(8,128)(2,1)} %get-tuple-element.91), channel_id=1, source_target_pairs={{4,0},{5,1},{6,2},{7,3},{8,4},{9,5},{10,6},{11,7},{12,8},{13,9},{1... | collective-permute-start | bytes 3145736 | tf_op jit(solution)/shard_map/ppermute | solution.py:35
  833.4 16.3 %copy-start.12 = (bf16[2,16,128,128]{2,3,0,1:T(8,128)(2,1)S(1)}, bf16[2,16,128,128]{2,3,0,1:T(8,128)(2,1)}, u32[]{:S(2)}) copy-start(bf16[2,16,128,128]{2,3,0,1:T(8,128)(2,1)} %get-tuple-element.107) | copy-start | bytes 3145732
  833.4 17.1 %copy-start.2 = (bf16[2,128,2048]{1,2,0:T(8,128)(2,1)S(1)}, bf16[2,128,2048]{1,2,0:T(8,128)(2,1)}, u32[]{:S(2)}) copy-start(bf16[2,128,2048]{1,2,0:T(8,128)(2,1)} %copy-done.1) | copy-start | bytes 3145732
  833.4 17.2 %copy-start.6 = (bf16[2,16,128,128]{2,3,0,1:T(8,128)(2,1)S(1)}, bf16[2,16,128,128]{2,3,0,1:T(8,128)(2,1)}, u32[]{:S(2)}) copy-start(bf16[2,16,128,128]{2,3,0,1:T(8,128)(2,1)} %fusion.34) | copy-start | bytes 3145732
  833.4 45.3 %collective-permute-start.12 = (bf16[128,4096]{1,0:T(8,128)(2,1)}, bf16[128,4096]{1,0:T(8,128)(2,1)}, u32[]{:S(2)}, u32[]{:S(2)}) collective-permute-start(bf16[128,4096]{1,0:T(8,128)(2,1)} %get-tuple-element.92), channel_id=1, source_target_pairs={{12,0},{13,1},{14,2},{15,3},{0,4},{1,5},{2,6},{3,7},{4,8},{5,9},{6... | collective-permute-start | bytes 3145736 | tf_op jit(solution)/shard_map/ppermute | solution.py:35
  840.8 37.9 %collective-permute-start.11 = (bf16[128,4096]{1,0:T(8,128)(2,1)}, bf16[128,4096]{1,0:T(8,128)(2,1)}, u32[]{:S(2)}, u32[]{:S(2)}) collective-permute-start(bf16[128,4096]{1,0:T(8,128)(2,1)} %get-tuple-element.93), channel_id=1, source_target_pairs={{2,0},{3,1},{4,2},{5,3},{6,4},{7,5},{8,6},{9,7},{10,8},{11,9},{12,... | collective-permute-start | bytes 3145736 | tf_op jit(solution)/shard_map/ppermute | solution.py:35
  846.1 66.1 %collective-permute-start.10 = (bf16[128,4096]{1,0:T(8,128)(2,1)}, bf16[128,4096]{1,0:T(8,128)(2,1)}, u32[]{:S(2)}, u32[]{:S(2)}) collective-permute-start(bf16[128,4096]{1,0:T(8,128)(2,1)} %get-tuple-element.94), channel_id=1, source_target_pairs={{14,0},{15,1},{0,2},{1,3},{2,4},{3,5},{4,6},{5,7},{6,8},{7,9},{8,1... | collective-permute-start | bytes 3145736 | tf_op jit(solution)/shard_map/ppermute | solution.py:35
  846.1 78.4 %collective-permute-start.9 = (bf16[128,4096]{1,0:T(8,128)(2,1)}, bf16[128,4096]{1,0:T(8,128)(2,1)}, u32[]{:S(2)}, u32[]{:S(2)}) collective-permute-start(bf16[128,4096]{1,0:T(8,128)(2,1)} %get-tuple-element.95), channel_id=1, source_target_pairs={{0,1},{1,2},{2,3},{3,4},{4,5},{5,6},{6,7},{7,8},{8,9},{9,10},{10,1... | collective-permute-start | bytes 3145736 | tf_op jit(solution)/shard_map/ppermute | solution.py:41
  858.7 3.6 copy-start.17
Sparse Core Ops, SparseCore 0:
  18.6 197.0 all-reduce.9
  300.8 143.3 all-reduce.5
  458.1 86.0 all-gather.1
  632.0 188.3 all-reduce.7
  858.8 43.4 reduce-scatter.1
where the time goes:
time: 950 us; the launch traced here: 940 us
  blocking collectives  311 us (33%)
  waiting for transfers between devices  242 us (25%)
  local copies, waits for them, and re-layouts  158 us (17%)
  other arithmetic  94.2 us (10%)
  matrix products  67.2 us (7%)
  starting transfers between devices  52.6 us (6%)
  between operations  14.6 us (2%)
    psum x1, blocking collectives, on_device(): lax.psum((edge_query_part, pool_terms[per_device + 2:per_device + 4]), 's...  183 us
    ppermute x12, waiting for transfers between devices, from_behind(): return lax.ppermute(block, axis, route)  182 us
    psum x1, blocking collectives, on_device(): lax.psum((jnp.sum(edge_exp, axis=3, keepdims=True), edge_part), 'seq')  64.9 us
    pmax x1, blocking collectives, on_device(): edge_max = lax.pmax(jnp.max(edge_scores, axis=3, keepdims=True), 'seq')  62.9 us
    scatter-add x1, other arithmetic, on_device(): pool_terms = jnp.zeros((pool_count, BLOCK, 2 * width), jnp.float32).at[po...  41.9 us
    ppermute x1, waiting for transfers between devices, extended(): lax.ppermute(lax.slice_in_dim(block, 0, width, axis=dim), axis, backward)  33.9 us
    unnamed x54, local copies, waits for them, and re-layouts  29.1 us
    ppermute x12, starting transfers between devices, from_behind(): return lax.ppermute(block, axis, route)  25.2 us
  transfers between devices with their start and end apart: 22, of which 10 were waited for; matrix products, arithmetic and copies ran while one was open for 29% of the time, Pallas kernels for 0%

commit v1 on v0

v1 whole, which is shorter than its diff:
```python
import functools
import math

import jax
import jax.numpy as jnp
from jax import lax
from jax.experimental import pallas as pl
from jax.experimental.pallas import tpu as pltpu
from jax.sharding import Mesh, PartitionSpec as P

HD = 128
BLOCK = 128
RAND = 3
SEQ = ("z1", "z0", "yh", "core")
NB = 16
SCALE = HD ** (-0.5)
VMEM_LIMIT = 48 * 1024 * 1024
EXP_SCALE = SCALE * math.log2(math.e)


def linked_blocks(block):
    if block in (0, NB - 1):
        return list(range(NB))
    seen = {block - 1, block, block + 1, 0, NB - 1}
    for step in range(RAND):
        shift = (step + 1) * (NB // (2 * RAND + 1))
        seen |= {(block + shift) % NB, (block - shift) % NB}
    return sorted(seen)


def dot(a, b, dims):
    return lax.dot_general(a, b, (dims, ((), ())), preferred_element_type=jnp.float32)


def attention_kernel(qkv, grad, d_qkv, attended, keys_t, values_t, d_keys, d_values):
    for c in range(NB):
        rows = slice(c * BLOCK, (c + 1) * BLOCK)
        keys_t[:, rows] = qkv[c, :, HD : 2 * HD].T
        values_t[:, rows] = qkv[c, :, 2 * HD :].T
    d_keys[...] = jnp.zeros_like(d_keys)
    d_values[...] = jnp.zeros_like(d_values)
    for b in range(NB):
        seen = linked_blocks(b)
        query = qkv[b, :, :HD]
        g = grad[b]
        keys = jnp.concatenate([qkv[c, :, HD : 2 * HD] for c in seen], axis=0)
        values = jnp.concatenate([qkv[c, :, 2 * HD :] for c in seen], axis=0)
        scores = dot(keys, query, ((1,), (1,)))
        prob_grad = dot(values, g, ((1,), (1,)))
        row_max = jnp.max(scores, axis=0, keepdims=True)
        weights = jnp.exp2((scores - row_max) * EXP_SCALE)
        inverse = 1.0 / jnp.sum(weights, axis=0, keepdims=True)
        v_t = jnp.concatenate([values_t[:, c * BLOCK : (c + 1) * BLOCK] for c in seen], axis=1)
        k_t = jnp.concatenate([keys_t[:, c * BLOCK : (c + 1) * BLOCK] for c in seen], axis=1)
        att = dot(v_t, weights.astype(jnp.bfloat16), ((1,), (0,))) * inverse
        attended[b] = att.astype(jnp.bfloat16)
        probs = weights * inverse
        delta = jnp.sum(probs * prob_grad, axis=0, keepdims=True)
        score_grad = (probs * (prob_grad - delta)).astype(jnp.bfloat16)
        probs = probs.astype(jnp.bfloat16)
        d_query = dot(k_t, score_grad, ((1,), (0,))) * SCALE
        d_qkv[b, :, :HD] = d_query.T.astype(jnp.bfloat16)
        key_term = dot(score_grad, query, ((1,), (0,)))
        value_term = dot(probs, g, ((1,), (0,)))
        for n, c in enumerate(seen):
            d_keys[c] += key_term[n * BLOCK : (n + 1) * BLOCK]
            d_values[c] += value_term[n * BLOCK : (n + 1) * BLOCK]
    for c in range(NB):
        d_qkv[c, :, HD : 2 * HD] = (d_keys[c] * SCALE).astype(jnp.bfloat16)
        d_qkv[c, :, 2 * HD :] = d_values[c].astype(jnp.bfloat16)


def attention(qkv, grad):
    vmem = pl.BlockSpec(memory_space=pltpu.VMEM)
    return pl.pallas_call(
        attention_kernel,
        out_shape=(
            jax.ShapeDtypeStruct((NB, BLOCK, 3 * HD), jnp.bfloat16),
            jax.ShapeDtypeStruct((NB, HD, BLOCK), jnp.bfloat16),
        ),
        in_specs=[vmem, vmem],
        out_specs=(vmem, vmem),
        scratch_shapes=[
            pltpu.VMEM((HD, NB * BLOCK), jnp.bfloat16),
            pltpu.VMEM((HD, NB * BLOCK), jnp.bfloat16),
            pltpu.VMEM((NB, BLOCK, HD), jnp.float32),
            pltpu.VMEM((NB, BLOCK, HD), jnp.float32),
        ],
        compiler_params=pltpu.CompilerParams(vmem_limit_bytes=VMEM_LIMIT),
        cost_estimate=pl.CostEstimate(flops=5_000_000_000, bytes_accessed=5_000_000, transcendentals=3_000_000),
        name="attention",
    )(qkv, grad)


def whole_call(kernel, out, name, *arrays, flops=0):
    vmem = pl.BlockSpec(memory_space=pltpu.VMEM)
    outs = out if isinstance(out, tuple) else (out,)
    moved = sum(x.size * x.dtype.itemsize for x in (*arrays, *outs))
    return pl.pallas_call(
        kernel,
        out_shape=out,
        in_specs=[vmem] * len(arrays),
        out_specs=jax.tree.map(lambda _: vmem, out),
        compiler_params=pltpu.CompilerParams(vmem_limit_bytes=VMEM_LIMIT),
        cost_estimate=pl.CostEstimate(flops=flops, bytes_accessed=moved, transcendentals=0),
        name=name,
    )(*arrays)


def pack_heads_kernel(rows, packed):
    heads = packed.shape[0]
    for h in range(heads):
        for kind in range(3):
            column = (kind * heads + h) * HD
            packed[h, :, kind * HD : (kind + 1) * HD] = rows[:, column : column + HD]


def unpack_heads_kernel(packed, rows):
    heads = packed.shape[0]
    for h in range(heads):
        for kind in range(3):
            column = (kind * heads + h) * HD
            rows[:, column : column + HD] = packed[h, :, kind * HD : (kind + 1) * HD]


def out_grad_kernel(up, w_out, grad):
    product = dot(up[...], w_out[...], ((1,), (1,)))
    for h in range(grad.shape[0]):
        grad[h] = product[:, h * HD : (h + 1) * HD].astype(jnp.bfloat16)


def out_grad_heads(up, w_out):
    tokens, width = up.shape
    step = 2 * HD
    return pl.pallas_call(
        out_grad_kernel,
        grid=(width // step,),
        out_shape=jax.ShapeDtypeStruct((width // HD, tokens, HD), jnp.bfloat16),
        in_specs=[
            pl.BlockSpec((tokens, width), lambda i: (0, 0)),
            pl.BlockSpec((step, width), lambda i: (i, 0)),
        ],
        out_specs=pl.BlockSpec((step // HD, tokens, HD), lambda i: (i, 0, 0)),
        compiler_params=pltpu.CompilerParams(vmem_limit_bytes=VMEM_LIMIT),
        cost_estimate=pl.CostEstimate(
            flops=2 * tokens * width * width, bytes_accessed=2 * width * width, transcendentals=0
        ),
        name="out_grad",
    )(up, w_out)


def pack_columns_kernel(up, packed):
    for block in range(up.shape[1] // HD):
        turned = up[:, block * HD : (block + 1) * HD].T
        for granule in range(8):
            z0, yh, core = granule // 4, granule // 2 % 2, granule % 2
            piece = turned[granule * 16 : (granule + 1) * 16]
            row = (block * 2 + yh) * 16
            for z1 in range(2):
                for yh_to in range(2):
                    packed[z1 * 8 + z0 * 4 + yh_to * 2 + core, row : row + 16, :] = piece


def tile_kernel(factor, columns, own, over_core, over_z, over_both, tile):
    blocks = range(NB)
    lhs = jnp.concatenate([columns[b] for b in blocks], axis=1)
    rhs = jnp.concatenate(
        [jnp.concatenate([part[b] for b in blocks], axis=1) for part in (own, over_core, over_z, over_both)],
        axis=0,
    )
    product = (dot(lhs, rhs, ((1,), (1,))) * factor).astype(jnp.bfloat16)
    for piece in range(tile.shape[0]):
        tile[piece] = product[piece * 16 : (piece + 1) * 16]


def combine_kernel(place, tiles, out):
    z0, core = place[0], place[1]
    for group in range(4):
        z1, yh = group // 2, group % 2
        total = tiles[group].astype(jnp.float32)
        for source in range(1, tiles.shape[0] // 4):
            total += tiles[source * 4 + group].astype(jnp.float32)
        for part in range(4):
            head = z1 * 8 + (z0 ^ (part // 2)) * 4 + yh * 2 + (core ^ (part % 2))
            start = pl.multiple_of(head * HD, HD)
            out[:, pl.ds(start, HD)] = total[:, part * HD : (part + 1) * HD]


def combine(place, tiles):
    vmem = pl.BlockSpec(memory_space=pltpu.VMEM)
    return pl.pallas_call(
        combine_kernel,
        out_shape=jax.ShapeDtypeStruct((tiles.shape[1], NB * HD), jnp.float32),
        in_specs=[pl.BlockSpec(memory_space=pltpu.SMEM), vmem],
        out_specs=vmem,
        compiler_params=pltpu.CompilerParams(vmem_limit_bytes=VMEM_LIMIT),
        name="combine",
    )(place, tiles)


def on_device(projected, upstream, w_out, partners):
    rows = projected[0]
    up = upstream[0]
    tokens = rows.shape[0]
    width = w_out.shape[0]
    heads = width // HD
    dp = lax.axis_size("dp")
    column_width = width // (dp * heads)
    factor = (tokens * heads * dp) ** (-0.5)
    shape = jax.ShapeDtypeStruct

    qkv = whole_call(pack_heads_kernel, shape((heads, tokens, 3 * HD), jnp.bfloat16), "pack_heads", rows)
    qkv = lax.all_to_all(qkv, SEQ, 0, 0, tiled=True)
    grad = lax.all_to_all(out_grad_heads(up, w_out), SEQ, 0, 0, tiled=True)
    columns = whole_call(
        pack_columns_kernel, shape((heads, width // 4, tokens), jnp.bfloat16), "pack_columns", up
    )
    columns = lax.all_to_all(columns, SEQ, 0, 0, tiled=True)

    d_qkv, attended = attention(qkv, grad)

    d_rows = lax.all_to_all(d_qkv, SEQ, 0, 0, tiled=True)
    d_rows = whole_call(unpack_heads_kernel, shape(rows.shape, jnp.bfloat16), "unpack_heads", d_rows)

    flip = [(0, 1), (1, 0)]
    over_z = lax.ppermute(attended, "z0", flip)
    over_core = lax.ppermute(attended, "core", flip)
    over_both = lax.ppermute(over_z, "core", flip)
    tile = whole_call(
        functools.partial(tile_kernel, factor),
        shape((dp * 4, column_width, 4 * HD), jnp.bfloat16),
        "tile",
        columns,
        attended,
        over_core,
        over_z,
        over_both,
        flops=2 * (width // 4) ** 2 * heads * tokens,
    )
    tile = lax.all_to_all(tile, ("dp", "z1", "yh"), 0, 0, tiled=True)
    place = jnp.stack([lax.axis_index("z0"), lax.axis_index("core")]).astype(jnp.int32)
    return d_rows[None], combine(place, tile).T


def solution(mesh):
    fine = Mesh(mesh.devices.reshape(-1, 2, 2, 2, 2), ("dp",) + SEQ)
    return jax.shard_map(
        on_device,
        mesh=fine,
        in_specs=(P("dp", SEQ, None), P("dp", SEQ, None), P(), P()),
        out_specs=(P("dp", SEQ, None), P(None, ("dp",) + SEQ)),
        check_vma=False,
    )
```

time: 950 us -> 157 us (0.17)
  the two profiles are of different devices: /device:TPU:24 before, /device:TPU:0 now
where the time goes in v1:
time: 157 us; the launch traced here: 156 us
  waiting for transfers between devices  83.6 us (53%)
  Pallas kernels  36.1 us (23%)
  starting transfers between devices  31.2 us (20%)
  local copies, waits for them, and re-layouts  4.73 us (3%)
    ppermute x1, waiting for transfers between devices, on_device(): over_z = lax.ppermute(attended, 'z0', flip)  29.4 us
    all_to_all x1, waiting for transfers between devices, on_device(): qkv = lax.all_to_all(qkv, SEQ, 0, 0, tiled=True)  22 us
    pallas_call x1, Pallas kernels, attention(): pl.pallas_call(attention_kernel, out_shape=(jax.ShapeDtypeStruct((NB, BLO...  18.1 us
    all_to_all x1, waiting for transfers between devices, on_device(): grad = lax.all_to_all(out_grad_heads(up, w_out), SEQ, 0, 0, tiled=True)  10.9 us
    all_to_all x1, waiting for transfers between devices, on_device(): tile = lax.all_to_all(tile, ('dp', 'z1', 'yh'), 0, 0, tiled=True)  10.8 us
    all_to_all x1, starting transfers between devices, on_device(): tile = lax.all_to_all(tile, ('dp', 'z1', 'yh'), 0, 0, tiled=True)  9.44 us
    all_to_all x1, waiting for transfers between devices, on_device(): columns = lax.all_to_all(columns, SEQ, 0, 0, tiled=True)  8.57 us
    pallas_call x1, Pallas kernels, out_grad_heads(): pl.pallas_call(out_grad_kernel, grid=(width // step,), out_shape=jax.Shap...  8.49 us
  transfers between devices with their start and end apart: 8, of which 6 were waited for; matrix products, arithmetic and copies ran while one was open for 0% of the time, Pallas kernels for 17%

profile of v1, /device:TPU:0, one launch (start us, length us, event | category | flops | bytes accessed | tf_op | source)
XLA Modules:
  0.0 156.4 jit_solution(6475741035272228937)
XLA Ops:
  0.6 0.0 copy-start
  0.6 1.0 copy-done
  1.7 0.0 copy-start.2
  1.7 8.5 %out_grad.1 = bf16[16,128,128]{2,1,0:T(8,128)(2,1)} custom-call(bf16[128,2048]{1,0:T(8,128)(2,1)S(1)} %bitcast.6, bf16[2048,2048]{1,0:T(8,128)(2,1)} %w_out.1), custom_call_target="tpu_custom_call" | custom-call | flops 1073741824 | bytes 8388608 | tf_op jit(solution)/shard_map/out_grad/pallas_call | solution.py:135
  10.2 8.1 %all-to-all-start.1 = ((bf16[16,128,128]{2,1,0:T(8,128)(2,1)}), bf16[16,128,128]{2,1,0:T(8,128)(2,1)S(1)}, u32[]{:S(2)}, u32[]{:S(2)}) async-start(bf16[16,128,128]{2,1,0:T(8,128)(2,1)} %out_grad.1), calls=%async_computation.1 | async-start | bytes 1048576 | tf_op jit(solution)/shard_map/all_to_all | solution.py:214
  18.3 0.0 copy-done.2
  18.3 1.4 pack_heads.1
  19.7 0.0 copy-start.1
  19.7 10.9 %all-to-all-done.1.grad = bf16[16,128,128]{2,1,0:T(8,128)(2,1)S(1)} async-done(((bf16[16,128,128]{2,1,0:T(8,128)(2,1)}), bf16[16,128,128]{2,1,0:T(8,128)(2,1)S(1)}, u32[]{:S(2)}, u32[]{:S(2)}) %all-to-all-start.1) | async-done | bytes 524320 | tf_op jit(solution)/shard_map/all_to_all | solution.py:214
  30.7 3.7 %all-to-all-start = ((bf16[16,128,384]{2,1,0:T(8,128)(2,1)}), bf16[16,128,384]{2,1,0:T(8,128)(2,1)S(1)}, u32[]{:S(2)}, u32[]{:S(2)}) async-start(bf16[16,128,384]{2,1,0:T(8,128)(2,1)} %pack_heads.1), calls=%async_computation | async-start | bytes 3145728 | tf_op jit(solution)/shard_map/all_to_all | solution.py:213
  34.4 0.0 copy-done.1
  34.4 1.7 %pack_columns.1 = bf16[16,512,128]{2,1,0:T(8,128)(2,1)} custom-call(bf16[128,2048]{1,0:T(8,128)(2,1)S(1)} %bitcast.7), custom_call_target="tpu_custom_call" | custom-call | bytes 2621440 | tf_op jit(solution)/shard_map/pack_columns/pallas_call | solution.py:99
  36.1 22.0 %all-to-all-done.qkv = bf16[16,128,384]{2,1,0:T(8,128)(2,1)S(1)} async-done(((bf16[16,128,384]{2,1,0:T(8,128)(2,1)}), bf16[16,128,384]{2,1,0:T(8,128)(2,1)S(1)}, u32[]{:S(2)}, u32[]{:S(2)}) %all-to-all-start) | async-done | bytes 1572896 | tf_op jit(solution)/shard_map/all_to_all | solution.py:213
  58.0 0.0 copy-start.4
  58.0 1.1 copy-done.4
  59.2 3.7 %all-to-all-start.3 = ((bf16[16,512,128]{2,1,0:T(8,128)(2,1)}), bf16[16,512,128]{2,1,0:T(8,128)(2,1)S(1)}, u32[]{:S(2)}, u32[]{:S(2)}) async-start(bf16[16,512,128]{2,1,0:T(8,128)(2,1)} %pack_columns.1), calls=%async_computation.3 | async-start | bytes 4194304 | tf_op jit(solution)/shard_map/all_to_all | solution.py:218
  62.9 0.0 copy-start.5
  62.9 1.4 copy-done.5
  64.3 18.1 %attention.1 = (bf16[16,128,384]{2,1,0:T(8,128)(2,1)S(1)}, bf16[16,128,128]{2,1,0:T(8,128)(2,1)S(1)}) custom-call(bf16[16,128,384]{2,1,0:T(8,128)(2,1)S(1)} %copy-done.5, bf16[16,128,128]{2,1,0:T(8,128)(2,1)S(1)} %all-to-all-done.1.grad), custom_call_target="tpu_custom_call" | custom-call | flops 5000000000 | bytes 5000000 | tf_op jit(solution)/shard_map/attention/pallas_call | solution.py:75
  82.5 0.0 copy-start.3
  82.5 1.1 copy-done.3
  83.6 8.6 %all-to-all-done.3.columns = bf16[16,512,128]{2,1,0:T(8,128)(2,1)S(1)} async-done(((bf16[16,512,128]{2,1,0:T(8,128)(2,1)}), bf16[16,512,128]{2,1,0:T(8,128)(2,1)S(1)}, u32[]{:S(2)}, u32[]{:S(2)}) %all-to-all-start.3) | async-done | bytes 2097184 | tf_op jit(solution)/shard_map/all_to_all | solution.py:218
  92.2 4.4 %all-to-all-start.2 = ((bf16[16,128,384]{2,1,0:T(8,128)(2,1)}), bf16[16,128,384]{2,1,0:T(8,128)(2,1)}, u32[]{:S(2)}, u32[]{:S(2)}) async-start(bf16[16,128,384]{2,1,0:T(8,128)(2,1)} %copy-done.3), calls=%async_computation.2 | async-start | bytes 3145728 | tf_op jit(solution)/shard_map/all_to_all | solution.py:222
  96.6 1.8 %collective-permute-start.1 = (bf16[16,128,128]{2,1,0:T(8,128)(2,1)S(1)}, bf16[16,128,128]{2,1,0:T(8,128)(2,1)S(1)}, u32[]{:S(2)}, u32[]{:S(2)}) collective-permute-start(bf16[16,128,128]{2,1,0:T(8,128)(2,1)S(1)} %get-tuple-element.5.own), channel_id=1, source_target_pairs={{0,4},{4,0},{1,5},{5,1},{2,6},{6,2},{3,7},{7,3},{8,12},{12,8},{9,1... | collective-permute-start | bytes 1572872 | tf_op jit(solution)/shard_map/ppermute | solution.py:226
  98.4 0.0 collective-permute-start
  98.4 29.4 %collective-permute-done.1.over_z = bf16[16,128,128]{2,1,0:T(8,128)(2,1)S(1)} collective-permute-done((bf16[16,128,128]{2,1,0:T(8,128)(2,1)S(1)}, bf16[16,128,128]{2,1,0:T(8,128)(2,1)S(1)}, u32[]{:S(2)}, u32[]{:S(2)}) %collective-permute-start.1) | collective-permute-done | bytes 524320 | tf_op jit(solution)/shard_map/ppermute | solution.py:226
  127.7 0.0 collective-permute-start.2
  127.7 0.0 collective-permute-done.over_core
  127.7 1.9 %collective-permute-done.2.over_both = bf16[16,128,128]{2,1,0:T(8,128)(2,1)S(1)} collective-permute-done((bf16[16,128,128]{2,1,0:T(8,128)(2,1)S(1)}, bf16[16,128,128]{2,1,0:T(8,128)(2,1)S(1)}, u32[]{:S(2)}, u32[]{:S(2)}) %collective-permute-start.2) | collective-permute-done | bytes 524320 | tf_op jit(solution)/shard_map/ppermute | solution.py:228
  129.7 2.1 %tile.1 = bf16[32,16,512]{2,1,0:T(8,128)(2,1)} custom-call(bf16[16,512,128]{2,1,0:T(8,128)(2,1)S(1)} %all-to-all-done.3.columns, bf16[16,128,128]{2,1,0:T(8,128)(2,1)S(1)} %get-tuple-element.5.own, bf16[16,128,128]{2,1,0:T(8,128)(2,1)S(1)} %collective-permute-done.over_core, bf16[16,128,128]{2,1,0:T(8,128)(2,1)S(1)} %collective-permute-done.1.over_z, ...), custom_call_target="tpu_custom_call" | custom-call | flops 1073741824 | bytes 4718592 | tf_op jit(solution)/shard_map/tile/pallas_call | solution.py:99
  131.8 0.0 all-to-all-done.2.packed
  131.8 9.4 %all-to-all-start.4 = ((bf16[32,16,512]{2,1,0:T(8,128)(2,1)}), bf16[32,16,512]{2,1,0:T(8,128)(2,1)S(1)}, u32[]{:S(2)}, u32[]{:S(2)}) async-start(bf16[32,16,512]{2,1,0:T(8,128)(2,1)} %tile.1), calls=%async_computation.4 | async-start | bytes 1048576 | tf_op jit(solution)/shard_map/all_to_all | solution.py:240
  141.2 0.1 pad_add_fusion.place
  141.3 3.0 %unpack_heads.1 = bf16[128,6144]{1,0:T(8,128)(2,1)} custom-call(bf16[16,128,384]{2,1,0:T(8,128)(2,1)} %all-to-all-done.2.packed), custom_call_target="tpu_custom_call" | custom-call | bytes 3145728 | tf_op jit(solution)/shard_map/unpack_heads/pallas_call | solution.py:99
  144.3 10.8 %all-to-all-done.4.tiles = bf16[32,16,512]{2,1,0:T(8,128)(2,1)S(1)} async-done(((bf16[32,16,512]{2,1,0:T(8,128)(2,1)}), bf16[32,16,512]{2,1,0:T(8,128)(2,1)S(1)}, u32[]{:S(2)}, u32[]{:S(2)}) %all-to-all-start.4) | async-done | bytes 524320 | tf_op jit(solution)/shard_map/all_to_all | solution.py:240
  155.1 1.3 combine.1
Async XLA Ops:
  0.6 1.0 copy-start
  1.7 16.6 %copy-start.2 = (bf16[1,128,6144]{2,1,0:T(8,128)(2,1)S(1)}, bf16[1,128,6144]{2,1,0:T(8,128)(2,1)}, u32[]{:S(2)}) copy-start(bf16[1,128,6144]{2,1,0:T(8,128)(2,1)} %param.4) | copy-start | bytes 4718596
  10.2 20.5 %all-to-all-start.1 = ((bf16[16,128,128]{2,1,0:T(8,128)(2,1)}), bf16[16,128,128]{2,1,0:T(8,128)(2,1)S(1)}, u32[]{:S(2)}, u32[]{:S(2)}) async-start(bf16[16,128,128]{2,1,0:T(8,128)(2,1)} %out_grad.1), calls=%async_computation.1 | async-start | bytes 1048576 | tf_op jit(solution)/shard_map/all_to_all | solution.py:214
  19.7 14.7 %copy-start.1 = (bf16[1,128,2048]{2,1,0:T(8,128)(2,1)S(1)}, bf16[1,128,2048]{2,1,0:T(8,128)(2,1)}, u32[]{:S(2)}) copy-start(bf16[1,128,2048]{2,1,0:T(8,128)(2,1)} %param.5) | copy-start | bytes 1572868
  30.7 27.4 %all-to-all-start = ((bf16[16,128,384]{2,1,0:T(8,128)(2,1)}), bf16[16,128,384]{2,1,0:T(8,128)(2,1)S(1)}, u32[]{:S(2)}, u32[]{:S(2)}) async-start(bf16[16,128,384]{2,1,0:T(8,128)(2,1)} %pack_heads.1), calls=%async_computation | async-start | bytes 3145728 | tf_op jit(solution)/shard_map/all_to_all | solution.py:213
  58.0 1.1 copy-start.4
  59.2 33.0 %all-to-all-start.3 = ((bf16[16,512,128]{2,1,0:T(8,128)(2,1)}), bf16[16,512,128]{2,1,0:T(8,128)(2,1)S(1)}, u32[]{:S(2)}, u32[]{:S(2)}) async-start(bf16[16,512,128]{2,1,0:T(8,128)(2,1)} %pack_columns.1), calls=%async_computation.3 | async-start | bytes 4194304 | tf_op jit(solution)/shard_map/all_to_all | solution.py:218
  62.9 1.4 copy-start.5
  82.5 1.1 copy-start.3
  92.2 39.6 %all-to-all-start.2 = ((bf16[16,128,384]{2,1,0:T(8,128)(2,1)}), bf16[16,128,384]{2,1,0:T(8,128)(2,1)}, u32[]{:S(2)}, u32[]{:S(2)}) async-start(bf16[16,128,384]{2,1,0:T(8,128)(2,1)} %copy-done.3), calls=%async_computation.2 | async-start | bytes 3145728 | tf_op jit(solution)/shard_map/all_to_all | solution.py:222
  96.6 31.2 %collective-permute-start.1 = (bf16[16,128,128]{2,1,0:T(8,128)(2,1)S(1)}, bf16[16,128,128]{2,1,0:T(8,128)(2,1)S(1)}, u32[]{:S(2)}, u32[]{:S(2)}) collective-permute-start(bf16[16,128,128]{2,1,0:T(8,128)(2,1)S(1)} %get-tuple-element.5.own), channel_id=1, source_target_pairs={{0,4},{4,0},{1,5},{5,1},{2,6},{6,2},{3,7},{7,3},{8,12},{12,8},{9,1... | collective-permute-start | bytes 1572872 | tf_op jit(solution)/shard_map/ppermute | solution.py:226
  98.4 29.4 %collective-permute-start = (bf16[16,128,128]{2,1,0:T(8,128)(2,1)S(1)}, bf16[16,128,128]{2,1,0:T(8,128)(2,1)S(1)}, u32[]{:S(2)}, u32[]{:S(2)}) collective-permute-start(bf16[16,128,128]{2,1,0:T(8,128)(2,1)S(1)} %get-tuple-element.5.own), channel_id=1, source_target_pairs={{0,1},{1,0},{2,3},{3,2},{4,5},{5,4},{6,7},{7,6},{8,9},{9,8},{10,11... | collective-permute-start | bytes 1572872 | tf_op jit(solution)/shard_map/ppermute | solution.py:227
  127.7 1.9 %collective-permute-start.2 = (bf16[16,128,128]{2,1,0:T(8,128)(2,1)S(1)}, bf16[16,128,128]{2,1,0:T(8,128)(2,1)S(1)}, u32[]{:S(2)}, u32[]{:S(2)}) collective-permute-start(bf16[16,128,128]{2,1,0:T(8,128)(2,1)S(1)} %collective-permute-done.1.over_z), channel_id=1, source_target_pairs={{0,1},{1,0},{2,3},{3,2},{4,5},{5,4},{6,7},{7,6},{8,9},{9,8},{10,11... | collective-permute-start | bytes 1572872 | tf_op jit(solution)/shard_map/ppermute | solution.py:228
  131.8 23.4 %all-to-all-start.4 = ((bf16[32,16,512]{2,1,0:T(8,128)(2,1)}), bf16[32,16,512]{2,1,0:T(8,128)(2,1)S(1)}, u32[]{:S(2)}, u32[]{:S(2)}) async-start(bf16[32,16,512]{2,1,0:T(8,128)(2,1)} %tile.1), calls=%async_computation.4 | async-start | bytes 1048576 | tf_op jit(solution)/shard_map/all_to_all | solution.py:240

commit v2 on v1

v2 whole, which is shorter than its diff:
```python
import functools
import math

import jax
import jax.numpy as jnp
from jax import lax
from jax.experimental import pallas as pl
from jax.experimental.pallas import tpu as pltpu
from jax.sharding import Mesh, PartitionSpec as P

HD = 128
BLOCK = 128
RAND = 3
DP = ("x", "ylo")
SEQ = ("z1", "z0", "yh", "core")
NB = 16
SCALE = HD ** (-0.5)
VMEM_LIMIT = 48 * 1024 * 1024
EXP_SCALE = SCALE * math.log2(math.e)


def linked_blocks(block):
    if block in (0, NB - 1):
        return list(range(NB))
    seen = {block - 1, block, block + 1, 0, NB - 1}
    for step in range(RAND):
        shift = (step + 1) * (NB // (2 * RAND + 1))
        seen |= {(block + shift) % NB, (block - shift) % NB}
    return sorted(seen)


def dot(a, b, dims):
    return lax.dot_general(a, b, (dims, ((), ())), preferred_element_type=jnp.float32)


def scores_of(qkv, block):
    seen = linked_blocks(block)
    keys = jnp.concatenate([qkv[c, :, HD : 2 * HD] for c in seen], axis=0)
    return seen, dot(keys, qkv[block, :, :HD], ((1,), (1,)))


def transposed(turned, seen):
    return jnp.concatenate([turned[:, c * BLOCK : (c + 1) * BLOCK] for c in seen], axis=1)


def forward_kernel(qkv, attended, stats, values_t):
    for c in range(NB):
        values_t[:, c * BLOCK : (c + 1) * BLOCK] = qkv[c, :, 2 * HD :].T
    for b in range(NB):
        seen, scores = scores_of(qkv, b)
        row_max = jnp.max(scores, axis=0, keepdims=True)
        weights = jnp.exp2((scores - row_max) * EXP_SCALE)
        inverse = 1.0 / jnp.sum(weights, axis=0, keepdims=True)
        att = dot(transposed(values_t, seen), weights.astype(jnp.bfloat16), ((1,), (0,)))
        attended[b] = (att * inverse).astype(jnp.bfloat16)
        stats[b] = jnp.concatenate([row_max, inverse], axis=0)


def backward_kernel(qkv, stats, d_qkv, keys_t, d_keys, d_values):
    for c in range(NB):
        keys_t[:, c * BLOCK : (c + 1) * BLOCK] = qkv[c, :, HD : 2 * HD].T
    d_keys[...] = jnp.zeros_like(d_keys)
    d_values[...] = jnp.zeros_like(d_values)
    for b in range(NB):
        seen, scores = scores_of(qkv, b)
        query = qkv[b, :, :HD]
        grad = qkv[b, :, 3 * HD :]
        values = jnp.concatenate([qkv[c, :, 2 * HD : 3 * HD] for c in seen], axis=0)
        prob_grad = dot(values, grad, ((1,), (1,)))
        probs = jnp.exp2((scores - stats[b, 0:1]) * EXP_SCALE) * stats[b, 1:2]
        delta = jnp.sum(probs * prob_grad, axis=0, keepdims=True)
        score_grad = (probs * (prob_grad - delta)).astype(jnp.bfloat16)
        d_query = dot(transposed(keys_t, seen), score_grad, ((1,), (0,))) * SCALE
        d_qkv[b, :, :HD] = d_query.T.astype(jnp.bfloat16)
        key_term = dot(score_grad, query, ((1,), (0,)))
        value_term = dot(probs.astype(jnp.bfloat16), grad, ((1,), (0,)))
        for n, c in enumerate(seen):
            d_keys[c] += key_term[n * BLOCK : (n + 1) * BLOCK]
            d_values[c] += value_term[n * BLOCK : (n + 1) * BLOCK]
    for c in range(NB):
        d_qkv[c, :, HD : 2 * HD] = (d_keys[c] * SCALE).astype(jnp.bfloat16)
        d_qkv[c, :, 2 * HD :] = d_values[c].astype(jnp.bfloat16)


def whole_call(kernel, out, name, *arrays, place=None, blocks=None, scratch=(), flops=0):
    blocks = blocks or {}

    def spec(x, block=None):
        shape, index = block or (x.shape, (0,) * len(x.shape))
        return pl.BlockSpec(shape, lambda i: index)

    moved = sum(x.size * x.dtype.itemsize for x in (*arrays, *jax.tree.leaves(out)))
    scalars = () if place is None else (place,)
    return pl.pallas_call(
        kernel,
        grid=(1,),
        out_shape=out,
        in_specs=[pl.BlockSpec(memory_space=pltpu.SMEM)] * len(scalars)
        + [spec(x, blocks.get(n)) for n, x in enumerate(arrays)],
        out_specs=jax.tree.map(spec, out),
        scratch_shapes=scratch,
        compiler_params=pltpu.CompilerParams(vmem_limit_bytes=VMEM_LIMIT),
        cost_estimate=pl.CostEstimate(flops=flops, bytes_accessed=moved, transcendentals=0),
        name=name,
    )(*scalars, *arrays)


def pack_kernel(up, w_out, queries, keys, values, packed, up_t):
    step = pl.program_id(0)

    @pl.when(step == 0)
    def _():
        for block in range(up.shape[1] // HD):
            columns = slice(block * HD, (block + 1) * HD)
            up_t[columns, :] = up[:, columns].T

    grad = dot(w_out[...], up_t[...], ((1,), (0,)))
    z0 = lax.rem(step // 2, 2)
    for core in range(2):
        columns = slice(core * HD, (core + 1) * HD)
        packed[core, :, :HD] = queries[:, columns]
        packed[core, :, HD : 2 * HD] = keys[:, columns]
        packed[core, :, 2 * HD : 3 * HD] = values[:, columns]
        packed[core, :, 3 * HD : 4 * HD] = grad[columns].T.astype(jnp.bfloat16)
        for granule in range(up.shape[1] // 64):
            start = pl.multiple_of(granule // 2 * 128 + z0 * 64 + granule % 2 * 32 + core * 16, 16)
            chunk, row = granule // 8, granule % 8 * 16
            packed[core, row : row + 16, (chunk + 4) * HD : (chunk + 5) * HD] = up_t[pl.ds(start, 16), :]


def pack(rows, up, w_out):
    tokens, width = up.shape
    step = 2 * HD
    steps = width // step
    return pl.pallas_call(
        pack_kernel,
        grid=(steps,),
        out_shape=jax.ShapeDtypeStruct((width // HD, tokens, 8 * HD), jnp.bfloat16),
        in_specs=[
            pl.BlockSpec((tokens, width), lambda i: (0, 0)),
            pl.BlockSpec((step, width), lambda i: (i, 0)),
            pl.BlockSpec((tokens, step), lambda i: (0, i)),
            pl.BlockSpec((tokens, step), lambda i: (0, steps + i)),
            pl.BlockSpec((tokens, step), lambda i: (0, 2 * steps + i)),
        ],
        out_specs=pl.BlockSpec((2, tokens, 8 * HD), lambda i: (i, 0, 0)),
        scratch_shapes=[pltpu.VMEM((width, tokens), jnp.bfloat16)],
        compiler_params=pltpu.CompilerParams(vmem_limit_bytes=VMEM_LIMIT),
        cost_estimate=pl.CostEstimate(
            flops=2 * tokens * width * width, bytes_accessed=2 * width * width, transcendentals=0
        ),
        name="pack",
    )(up, w_out, rows, rows, rows)


def unpack_heads_kernel(packed, rows):
    heads = packed.shape[0]
    for h in range(heads):
        for kind in range(3):
            column = (kind * heads + h) * HD
            rows[:, column : column + HD] = packed[h, :, kind * HD : (kind + 1) * HD]


def tile_kernel(factor, place, columns, own, over_core, over_z, over_both, *outs):
    *outs, product = outs
    blocks = range(NB)
    lhs = jnp.concatenate(
        [
            jnp.concatenate([columns[b, :, chunk * HD : (chunk + 1) * HD] for b in blocks], axis=1)
            for chunk in range(4)
        ],
        axis=0,
    )
    rhs = jnp.concatenate(
        [jnp.concatenate([part[b] for b in blocks], axis=1) for part in (own, over_core, over_z, over_both)],
        axis=0,
    )
    product[...] = dot(lhs, rhs, ((1,), (1,))) * factor
    rows = outs[0].shape[0]
    for far, out in enumerate(outs):
        to = lax.rem(place[2] + far, len(outs))
        out[...] = product[pl.ds(pl.multiple_of(to * rows, rows), rows), :].astype(out.dtype)


def sum_kernel(place, *refs):
    tiles, outs, total = refs[:4], refs[4:-1], refs[-1]
    value = tiles[0][...].astype(jnp.float32)
    for tile in tiles[1:]:
        value += tile[...].astype(jnp.float32)
    total[...] = value
    rows = outs[0].shape[0]
    for far, out in enumerate(outs):
        to = place[3] ^ far
        out[...] = total[pl.ds(pl.multiple_of(to * rows, rows), rows), :]


def combine_kernel(place, *refs):
    *parts, out = refs
    for far in range(4):
        source = place[3] ^ far
        z1, yh = lax.rem(source // 2, 2), lax.rem(source, 2)
        total = parts[far][...] + parts[far + 4][...]
        for near in range(4):
            head = z1 * 8 + (place[0] ^ (near // 2)) * 4 + yh * 2 + (place[1] ^ (near % 2))
            start = pl.multiple_of(head * HD, HD)
            out[:, pl.ds(start, HD)] = total[:, near * HD : (near + 1) * HD]


def on_device(projected, upstream, w_out, partners):
    rows = projected[0]
    up = upstream[0]
    tokens = rows.shape[0]
    width = w_out.shape[0]
    heads = width // HD
    dp = lax.axis_size("x") * lax.axis_size("ylo")
    column_width = width // (dp * heads)
    factor = (tokens * heads * dp) ** (-0.5)
    shape = jax.ShapeDtypeStruct
    eight = ("ylo", "z1", "yh")
    place = jnp.stack([lax.axis_index(a) for a in ("z0", "core", "x", eight)]).astype(jnp.int32)

    packed = lax.all_to_all(pack(rows, up, w_out), SEQ, 0, 0, tiled=True)
    attended, stats = whole_call(
        forward_kernel,
        (shape((NB, HD, BLOCK), jnp.bfloat16), shape((NB, 2, BLOCK), jnp.float32)),
        "forward",
        packed,
        blocks={0: ((NB, BLOCK, 3 * HD), (0, 0, 0))},
        scratch=[pltpu.VMEM((HD, NB * BLOCK), jnp.bfloat16)],
        flops=2_000_000_000,
    )
    flip = [(0, 1), (1, 0)]
    over_z = lax.ppermute(attended, "z0", flip)
    over_core = lax.ppermute(attended, "core", flip)
    d_qkv = whole_call(
        backward_kernel,
        shape((NB, BLOCK, 3 * HD), jnp.bfloat16),
        "backward",
        packed,
        stats,
        blocks={0: ((NB, BLOCK, 4 * HD), (0, 0, 0))},
        scratch=[
            pltpu.VMEM((HD, NB * BLOCK), jnp.bfloat16),
            pltpu.VMEM((NB, BLOCK, HD), jnp.float32),
            pltpu.VMEM((NB, BLOCK, HD), jnp.float32),
        ],
        flops=4_000_000_000,
    )
    d_qkv, over_z, over_core = lax.optimization_barrier((d_qkv, over_z, over_core))
    over_both = lax.ppermute(over_z, "core", flip)
    d_rows = lax.all_to_all(d_qkv, SEQ, 0, 0, tiled=True)

    tiles = whole_call(
        functools.partial(tile_kernel, factor),
        (shape((width // 16, 4 * HD), jnp.bfloat16),) * 4,
        "tile",
        packed,
        attended,
        over_core,
        over_z,
        over_both,
        place=place,
        blocks={0: ((NB, BLOCK, 4 * HD), (0, 0, 1))},
        scratch=[pltpu.VMEM((width // 4, 4 * HD), jnp.float32)],
        flops=2 * (width // 4) ** 2 * heads * tokens,
    )
    tiles = [tiles[0]] + [
        lax.ppermute(tiles[far], "x", [(i, (i + far) % 4) for i in range(4)]) for far in range(1, 4)
    ]
    parts = whole_call(
        sum_kernel,
        (shape((column_width, 4 * HD), jnp.float32),) * 8,
        "sum_tiles",
        *tiles,
        place=place,
        scratch=[pltpu.VMEM((width // 16, 4 * HD), jnp.float32)],
    )
    parts = [parts[0]] + [lax.ppermute(parts[far], eight, [(i, i ^ far) for i in range(8)]) for far in range(1, 8)]
    grad_w_out = whole_call(
        combine_kernel, shape((column_width, width), jnp.float32), "combine", *parts, place=place
    )
    d_rows = whole_call(unpack_heads_kernel, shape(rows.shape, jnp.bfloat16), "unpack_heads", d_rows)
    return d_rows[None], grad_w_out.T


def solution(mesh):
    fine = Mesh(mesh.devices.reshape(4, 2, 2, 2, 2, 2), DP + SEQ)
    return jax.shard_map(
        on_device,
        mesh=fine,
        in_specs=(P(DP, SEQ, None), P(DP, SEQ, None), P(), P()),
        out_specs=(P(DP, SEQ, None), P(None, DP + SEQ)),
        check_vma=False,
    )
```

time: 157 us -> 135 us (0.86)
  waiting for transfers between devices: 83.6 us -> 13.7 us
  blocking collectives: 0 us -> 59.8 us
  starting transfers between devices: 31.2 us -> 24.1 us
  Pallas kernels: 36.1 us -> 33.4 us
  local copies, waits for them, and re-layouts: 4.73 us -> 2.45 us
    all_to_all x0 -> x1, blocking collectives: none -> 59.8 us  [on_device(): packed = lax.all_to_all(pack(rows, up, w_out), SEQ, 0, 0, tiled=True)]
    all_to_all x4 -> x0, waiting for transfers between devices: 52.3 us -> none  [the longest x1 22 us: on_device(): qkv = lax.all_to_all(qkv, SEQ, 0, 0, tiled=True)]
    ppermute x1, waiting for transfers between devices: 29.4 us -> 0.62 us  [on_device(): over_z = lax.ppermute(attended, 'z0', flip)]
    all_to_all x4 -> x0, starting transfers between devices: 25 us -> none  [the longest x1 9.44 us: on_device(): tile = lax.all_to_all(tile, ('dp', 'z1', 'yh'), 0, 0, tiled=True)]
    ppermute x0 -> x10, starting transfers between devices: none -> 19.8 us  [the longest x7 14.1 us: on_device(): lax.ppermute(parts[far], eight, [(i, i ^ far) for i in range(8)])]
    ppermute x0 -> x10, waiting for transfers between devices: none -> 11.3 us  [the longest x7 6.36 us: on_device(): lax.ppermute(parts[far], eight, [(i, i ^ far) for i in range(8)])]
    pallas_call x7, Pallas kernels: 36.1 us -> 33.4 us  [the longest x6 24 us: whole_call(): pl.pallas_call(kernel, grid=(1,), out_shape=out, in_specs=[pl.BlockSpec(m...]
    unnamed x12 -> x6, local copies, waits for them, and re-layouts: 4.73 us -> 2.45 us
  transfers between devices with their start and end apart: 8 -> 14, of which waited for: 6 -> 6; matrix products, arithmetic and copies ran while one was open for 0% -> 0% of each run, Pallas kernels for 17% -> 13%
where the time goes in v2:
time: 135 us; the launch traced here: 134 us
  blocking collectives  59.8 us (44%)
  Pallas kernels  33.4 us (25%)
  starting transfers between devices  24.1 us (18%)
  waiting for transfers between devices  13.7 us (10%)
  local copies, waits for them, and re-layouts  2.45 us (2%)
    all_to_all x1, blocking collectives, on_device(): packed = lax.all_to_all(pack(rows, up, w_out), SEQ, 0, 0, tiled=True)  59.8 us
    pallas_call x6, Pallas kernels, whole_call(): pl.pallas_call(kernel, grid=(1,), out_shape=out, in_specs=[pl.BlockSpec(m...  24 us
    ppermute x7, starting transfers between devices, on_device(): lax.ppermute(parts[far], eight, [(i, i ^ far) for i in range(8)])  14.1 us
    pallas_call x1, Pallas kernels, pack(): pl.pallas_call(pack_kernel, grid=(steps,), out_shape=jax.ShapeDtypeStruct...  9.39 us
    ppermute x7, waiting for transfers between devices, on_device(): lax.ppermute(parts[far], eight, [(i, i ^ far) for i in range(8)])  6.36 us
    ppermute x3, starting transfers between devices, on_device(): lax.ppermute(tiles[far], 'x', [(i, (i + far) % 4) for i in range(4)])  5.72 us
    ppermute x3, waiting for transfers between devices, on_device(): lax.ppermute(tiles[far], 'x', [(i, (i + far) % 4) for i in range(4)])  4.96 us
    all_to_all x1, starting transfers between devices, on_device(): d_rows = lax.all_to_all(d_qkv, SEQ, 0, 0, tiled=True)  3.71 us
  transfers between devices with their start and end apart: 14, of which 6 were waited for; matrix products, arithmetic and copies ran while one was open for 0% of the time, Pallas kernels for 13%

profile of v2, /device:TPU:0, one launch (start us, length us, event | category | flops | bytes accessed | tf_op | source)
XLA Modules:
  0.0 134.3 jit_solution(8612866797070392966)
XLA Ops:
  0.6 0.0 copy-start.1
  0.6 1.4 %copy-done.1 = bf16[1,128,6144]{2,1,0:T(8,128)(2,1)S(1)} copy-done((bf16[1,128,6144]{2,1,0:T(8,128)(2,1)S(1)}, bf16[1,128,6144]{2,1,0:T(8,128)(2,1)}, u32[]{:S(2)}) %copy-start.1) | copy-done | bytes 1572888
  2.0 0.0 copy-start.2
  2.0 1.0 copy-done.2
  3.1 9.4 %pack.1 = bf16[16,128,1024]{2,1,0:T(8,128)(2,1)} custom-call(bf16[128,2048]{1,0:T(8,128)(2,1)S(1)} %bitcast.11, bf16[2048,2048]{1,0:T(8,128)(2,1)} %w_out.1, bf16[128,6144]{1,0:T(8,128)(2,1)S(1)} %bitcast.8, bf16[128,6144]{1,0:T(8,128)(2,1)S(1)} %bitcast.9, bf16[128,6144]{1,0:T(8,128)(2,1)S(1)} %bitcast.10), custom_call_target="tpu_custom_call" | custom-call | flops 1073741824 | bytes 8388608 | tf_op jit(solution)/shard_map/pack/pallas_call | solution.py:135
  12.5 59.8 %all_to_all.10.qkv.columns = bf16[16,128,1024]{2,1,0:T(8,128)(2,1)S(1)} all-to-all(bf16[16,128,1024]{2,1,0:T(8,128)(2,1)} %pack.1), channel_id=1, replica_groups=mesh['x'=4,'ylo'=2,'z1'=2,'z0'=2,'yh'=2,'core'=2] {'z1','z0','yh','core'}, dimensions={0} | all-to-all | bytes 8388608 | tf_op jit(solution)/shard_map/all_to_all | solution.py:222
  72.3 0.0 copy-start
  72.3 5.2 %forward.1 = (bf16[16,128,128]{2,1,0:T(8,128)(2,1)S(1)}, f32[16,2,128]{2,1,0:T(2,128)S(1)}) custom-call(bf16[16,128,1024]{2,1,0:T(8,128)(2,1)S(1)} %all_to_all.10.qkv.columns), custom_call_target="tpu_custom_call" | custom-call | flops 2000000000 | bytes 4734976 | tf_op jit(solution)/shard_map/forward/pallas_call | solution.py:94
  77.5 0.1 collective-permute-start
  77.6 0.3 collective-permute-start.1
  77.9 0.0 copy-done
  77.9 12.3 %backward.1 = bf16[16,128,384]{2,1,0:T(8,128)(2,1)} custom-call(bf16[16,128,1024]{2,1,0:T(8,128)(2,1)S(1)} %all_to_all.10.qkv.columns, f32[16,2,128]{2,1,0:T(2,128)S(1)} %get-tuple-element.19.stats), custom_call_target="tpu_custom_call" | custom-call | flops 4000000000 | bytes 5783552 | tf_op jit(solution)/shard_map/backward/pallas_call | solution.py:94
  90.1 0.6 collective-permute-done.over_z
  90.7 0.0 collective-permute-done.1.over_core
  90.7 3.7 %all-to-all-start.1 = ((bf16[16,128,384]{2,1,0:T(8,128)(2,1)}), bf16[16,128,384]{2,1,0:T(8,128)(2,1)S(1)}, u32[]{:S(2)}, u32[]{:S(2)}) async-start(bf16[16,128,384]{2,1,0:T(8,128)(2,1)} %backward.1), calls=%async_computation.1 | async-start | bytes 3145728 | tf_op jit(solution)/shard_map/all_to_all | solution.py:251
  94.5 0.3 collective-permute-start.2
  94.8 0.1 pad_add_fusion.place
  94.8 1.8 %collective-permute-done.2.over_both = bf16[16,128,128]{2,1,0:T(8,128)(2,1)} collective-permute-done((bf16[16,128,128]{2,1,0:T(8,128)(2,1)S(1)}, bf16[16,128,128]{2,1,0:T(8,128)(2,1)}, u32[]{:S(2)}, u32[]{:S(2)}) %collective-permute-start.2) | collective-permute-done | bytes 524320 | tf_op jit(solution)/shard_map/ppermute | solution.py:250
  96.6 3.1 %tile.1 = (bf16[128,512]{1,0:T(8,128)(2,1)S(1)}, bf16[128,512]{1,0:T(8,128)(2,1)S(1)}, bf16[128,512]{1,0:T(8,128)(2,1)S(1)}, bf16[128,512]{1,0:T(8,128)(2,1)S(1)}) custom-call(s32[4]{0:T(128)S(1)} %pad_add_fusion.place, bf16[16,128,1024]{2,1,0:T(8,128)(2,1)} %copy-done, bf16[16,128,128]{2,1,0:T(8,128)(2,1)S(1)} %get-tuple-element.20.own, ...), custom_call_target="tpu_custom_call" | custom-call | flops 1073741824 | bytes 6815744 | tf_op jit(solution)/shard_map/tile/pallas_call | solution.py:94
  99.7 1.6 %collective-permute-start.3 = (bf16[128,512]{1,0:T(8,128)(2,1)S(1)}, bf16[128,512]{1,0:T(8,128)(2,1)S(1)}, u32[]{:S(2)}, u32[]{:S(2)}) collective-permute-start(bf16[128,512]{1,0:T(8,128)(2,1)S(1)} %get-tuple-element.25), channel_id=1, source_target_pairs={{0,32},{32,64},{64,96},{96,0},{1,33},{33,65},{65,97},{97,1},{2,34}... | collective-permute-start | bytes 393224 | tf_op jit(solution)/shard_map/ppermute | solution.py:268
  101.2 2.7 %collective-permute-start.4 = (bf16[128,512]{1,0:T(8,128)(2,1)S(1)}, bf16[128,512]{1,0:T(8,128)(2,1)S(1)}, u32[]{:S(2)}, u32[]{:S(2)}) collective-permute-start(bf16[128,512]{1,0:T(8,128)(2,1)S(1)} %get-tuple-element.26), channel_id=1, source_target_pairs={{0,64},{32,96},{64,0},{96,32},{1,65},{33,97},{65,1},{97,33},{2,66}... | collective-permute-start | bytes 393224 | tf_op jit(solution)/shard_map/ppermute | solution.py:268
  103.9 1.4 %collective-permute-start.5 = (bf16[128,512]{1,0:T(8,128)(2,1)S(1)}, bf16[128,512]{1,0:T(8,128)(2,1)S(1)}, u32[]{:S(2)}, u32[]{:S(2)}) collective-permute-start(bf16[128,512]{1,0:T(8,128)(2,1)S(1)} %get-tuple-element.27), channel_id=1, source_target_pairs={{0,96},{32,0},{64,32},{96,64},{1,97},{33,1},{65,33},{97,65},{2,98}... | collective-permute-start | bytes 393224 | tf_op jit(solution)/shard_map/ppermute | solution.py:268
  105.4 1.2 collective-permute-done.3.refs_1_
  106.5 3.8 %collective-permute-done.4.refs_2_ = bf16[128,512]{1,0:T(8,128)(2,1)S(1)} collective-permute-done((bf16[128,512]{1,0:T(8,128)(2,1)S(1)}, bf16[128,512]{1,0:T(8,128)(2,1)S(1)}, u32[]{:S(2)}, u32[]{:S(2)}) %collective-permute-start.4) | collective-permute-done | bytes 131104 | tf_op jit(solution)/shard_map/ppermute | solution.py:268
  110.3 0.0 collective-permute-done.5.refs_3_
  110.3 0.6 sum_tiles.1
  111.0 3.1 %collective-permute-start.10 = (f32[16,512]{1,0:T(8,128)S(1)}, f32[16,512]{1,0:T(8,128)S(1)}, u32[]{:S(2)}, u32[]{:S(2)}) collective-permute-start(f32[16,512]{1,0:T(8,128)S(1)} %get-tuple-element.33), channel_id=1, source_target_pairs={{0,18},{2,16},{8,26},{10,24},{16,2},{18,0},{24,10},{26,8},{1,19},{... | collective-permute-start | bytes 98312 | tf_op jit(solution)/shard_map/ppermute | solution.py:278
  114.1 2.6 %collective-permute-start.11 = (f32[16,512]{1,0:T(8,128)S(1)}, f32[16,512]{1,0:T(8,128)S(1)}, u32[]{:S(2)}, u32[]{:S(2)}) collective-permute-start(f32[16,512]{1,0:T(8,128)S(1)} %get-tuple-element.34), channel_id=1, source_target_pairs={{0,24},{2,26},{8,16},{10,18},{16,8},{18,10},{24,0},{26,2},{1,25},{... | collective-permute-start | bytes 98312 | tf_op jit(solution)/shard_map/ppermute | solution.py:278
  116.7 0.6 collective-permute-start.12
  117.3 3.3 %collective-permute-start.6 = (f32[16,512]{1,0:T(8,128)S(1)}, f32[16,512]{1,0:T(8,128)S(1)}, u32[]{:S(2)}, u32[]{:S(2)}) collective-permute-start(f32[16,512]{1,0:T(8,128)S(1)} %get-tuple-element.29), channel_id=1, source_target_pairs={{0,2},{2,0},{8,10},{10,8},{16,18},{18,16},{24,26},{26,24},{1,3},{3... | collective-permute-start | bytes 98312 | tf_op jit(solution)/shard_map/ppermute | solution.py:278
  120.6 3.0 %collective-permute-start.7 = (f32[16,512]{1,0:T(8,128)S(1)}, f32[16,512]{1,0:T(8,128)S(1)}, u32[]{:S(2)}, u32[]{:S(2)}) collective-permute-start(f32[16,512]{1,0:T(8,128)S(1)} %get-tuple-element.30), channel_id=1, source_target_pairs={{0,8},{2,10},{8,0},{10,2},{16,24},{18,26},{24,16},{26,18},{1,9},{3... | collective-permute-start | bytes 98312 | tf_op jit(solution)/shard_map/ppermute | solution.py:278
  123.6 0.0 collective-permute-done.10.refs_5_
  123.6 0.2 collective-permute-start.8
  123.8 0.0 collective-permute-done.11.refs_6_
  123.8 1.3 collective-permute-start.9
  125.1 0.0 collective-permute-done.12.refs_7_
  125.1 0.0 collective-permute-done.6.refs_1_
  125.1 0.9 collective-permute-done.7.refs_2_
  126.0 5.4 %collective-permute-done.8.refs_3_ = f32[16,512]{1,0:T(8,128)S(1)} collective-permute-done((f32[16,512]{1,0:T(8,128)S(1)}, f32[16,512]{1,0:T(8,128)S(1)}, u32[]{:S(2)}, u32[]{:S(2)}) %collective-permute-start.8) | collective-permute-done | bytes 32800 | tf_op jit(solution)/shard_map/ppermute | solution.py:278
  131.4 0.0 collective-permute-done.9.refs_4_
  131.4 1.3 combine.1
  132.7 0.0 all-to-all-done.1.packed
  132.7 1.6 %unpack_heads.1 = bf16[128,6144]{1,0:T(8,128)(2,1)} custom-call(bf16[16,128,384]{2,1,0:T(8,128)(2,1)S(1)} %all-to-all-done.1.packed), custom_call_target="tpu_custom_call" | custom-call | bytes 3145728 | tf_op jit(solution)/shard_map/unpack_heads/pallas_call | solution.py:94
Async XLA Ops:
  0.6 1.4 %copy-start.1 = (bf16[1,128,6144]{2,1,0:T(8,128)(2,1)S(1)}, bf16[1,128,6144]{2,1,0:T(8,128)(2,1)}, u32[]{:S(2)}) copy-start(bf16[1,128,6144]{2,1,0:T(8,128)(2,1)} %param.4) | copy-start | bytes 4718596
  2.0 1.0 copy-start.2
  72.3 5.6 %copy-start = (bf16[16,128,1024]{2,1,0:T(8,128)(2,1)}, bf16[16,128,1024]{2,1,0:T(8,128)(2,1)S(1)}, u32[]{:S(2)}) copy-start(bf16[16,128,1024]{2,1,0:T(8,128)(2,1)S(1)} %all_to_all.10.qkv.columns) | copy-start | bytes 12582916
  77.5 13.3 %collective-permute-start = (bf16[16,128,128]{2,1,0:T(8,128)(2,1)S(1)}, bf16[16,128,128]{2,1,0:T(8,128)(2,1)S(1)}, u32[]{:S(2)}, u32[]{:S(2)}) collective-permute-start(bf16[16,128,128]{2,1,0:T(8,128)(2,1)S(1)} %get-tuple-element.20.own), channel_id=1, source_target_pairs={{0,4},{4,0},{1,5},{5,1},{2,6},{6,2},{3,7},{7,3},{8,12},{12,8},{9,1... | collective-permute-start | bytes 1572872 | tf_op jit(solution)/shard_map/ppermute | solution.py:233
  77.6 13.2 %collective-permute-start.1 = (bf16[16,128,128]{2,1,0:T(8,128)(2,1)S(1)}, bf16[16,128,128]{2,1,0:T(8,128)(2,1)S(1)}, u32[]{:S(2)}, u32[]{:S(2)}) collective-permute-start(bf16[16,128,128]{2,1,0:T(8,128)(2,1)S(1)} %get-tuple-element.20.own), channel_id=1, source_target_pairs={{0,1},{1,0},{2,3},{3,2},{4,5},{5,4},{6,7},{7,6},{8,9},{9,8},{10,11... | collective-permute-start | bytes 1572872 | tf_op jit(solution)/shard_map/ppermute | solution.py:234
  90.7 41.9 %all-to-all-start.1 = ((bf16[16,128,384]{2,1,0:T(8,128)(2,1)}), bf16[16,128,384]{2,1,0:T(8,128)(2,1)S(1)}, u32[]{:S(2)}, u32[]{:S(2)}) async-start(bf16[16,128,384]{2,1,0:T(8,128)(2,1)} %backward.1), calls=%async_computation.1 | async-start | bytes 3145728 | tf_op jit(solution)/shard_map/all_to_all | solution.py:251
  94.5 2.1 %collective-permute-start.2 = (bf16[16,128,128]{2,1,0:T(8,128)(2,1)S(1)}, bf16[16,128,128]{2,1,0:T(8,128)(2,1)}, u32[]{:S(2)}, u32[]{:S(2)}) collective-permute-start(bf16[16,128,128]{2,1,0:T(8,128)(2,1)S(1)} %collective-permute-done.over_z), channel_id=1, source_target_pairs={{0,1},{1,0},{2,3},{3,2},{4,5},{5,4},{6,7},{7,6},{8,9},{9,8},{10,11... | collective-permute-start | bytes 1572872 | tf_op jit(solution)/shard_map/ppermute | solution.py:250
  99.7 6.9 %collective-permute-start.3 = (bf16[128,512]{1,0:T(8,128)(2,1)S(1)}, bf16[128,512]{1,0:T(8,128)(2,1)S(1)}, u32[]{:S(2)}, u32[]{:S(2)}) collective-permute-start(bf16[128,512]{1,0:T(8,128)(2,1)S(1)} %get-tuple-element.25), channel_id=1, source_target_pairs={{0,32},{32,64},{64,96},{96,0},{1,33},{33,65},{65,97},{97,1},{2,34}... | collective-permute-start | bytes 393224 | tf_op jit(solution)/shard_map/ppermute | solution.py:268
  101.2 9.1 %collective-permute-start.4 = (bf16[128,512]{1,0:T(8,128)(2,1)S(1)}, bf16[128,512]{1,0:T(8,128)(2,1)S(1)}, u32[]{:S(2)}, u32[]{:S(2)}) collective-permute-start(bf16[128,512]{1,0:T(8,128)(2,1)S(1)} %get-tuple-element.26), channel_id=1, source_target_pairs={{0,64},{32,96},{64,0},{96,32},{1,65},{33,97},{65,1},{97,33},{2,66}... | collective-permute-start | bytes 393224 | tf_op jit(solution)/shard_map/ppermute | solution.py:268
  103.9 6.4 %collective-permute-start.5 = (bf16[128,512]{1,0:T(8,128)(2,1)S(1)}, bf16[128,512]{1,0:T(8,128)(2,1)S(1)}, u32[]{:S(2)}, u32[]{:S(2)}) collective-permute-start(bf16[128,512]{1,0:T(8,128)(2,1)S(1)} %get-tuple-element.27), channel_id=1, source_target_pairs={{0,96},{32,0},{64,32},{96,64},{1,97},{33,1},{65,33},{97,65},{2,98}... | collective-permute-start | bytes 393224 | tf_op jit(solution)/shard_map/ppermute | solution.py:268
  111.0 12.6 %collective-permute-start.10 = (f32[16,512]{1,0:T(8,128)S(1)}, f32[16,512]{1,0:T(8,128)S(1)}, u32[]{:S(2)}, u32[]{:S(2)}) collective-permute-start(f32[16,512]{1,0:T(8,128)S(1)} %get-tuple-element.33), channel_id=1, source_target_pairs={{0,18},{2,16},{8,26},{10,24},{16,2},{18,0},{24,10},{26,8},{1,19},{... | collective-permute-start | bytes 98312 | tf_op jit(solution)/shard_map/ppermute | solution.py:278
  114.1 9.7 %collective-permute-start.11 = (f32[16,512]{1,0:T(8,128)S(1)}, f32[16,512]{1,0:T(8,128)S(1)}, u32[]{:S(2)}, u32[]{:S(2)}) collective-permute-start(f32[16,512]{1,0:T(8,128)S(1)} %get-tuple-element.34), channel_id=1, source_target_pairs={{0,24},{2,26},{8,16},{10,18},{16,8},{18,10},{24,0},{26,2},{1,25},{... | collective-permute-start | bytes 98312 | tf_op jit(solution)/shard_map/ppermute | solution.py:278
  116.7 8.4 %collective-permute-start.12 = (f32[16,512]{1,0:T(8,128)S(1)}, f32[16,512]{1,0:T(8,128)S(1)}, u32[]{:S(2)}, u32[]{:S(2)}) collective-permute-start(f32[16,512]{1,0:T(8,128)S(1)} %get-tuple-element.35), channel_id=1, source_target_pairs={{0,26},{2,24},{8,18},{10,16},{16,10},{18,8},{24,2},{26,0},{1,27},{... | collective-permute-start | bytes 98312 | tf_op jit(solution)/shard_map/ppermute | solution.py:278
  117.3 7.8 %collective-permute-start.6 = (f32[16,512]{1,0:T(8,128)S(1)}, f32[16,512]{1,0:T(8,128)S(1)}, u32[]{:S(2)}, u32[]{:S(2)}) collective-permute-start(f32[16,512]{1,0:T(8,128)S(1)} %get-tuple-element.29), channel_id=1, source_target_pairs={{0,2},{2,0},{8,10},{10,8},{16,18},{18,16},{24,26},{26,24},{1,3},{3... | collective-permute-start | bytes 98312 | tf_op jit(solution)/shard_map/ppermute | solution.py:278
  120.6 5.4 %collective-permute-start.7 = (f32[16,512]{1,0:T(8,128)S(1)}, f32[16,512]{1,0:T(8,128)S(1)}, u32[]{:S(2)}, u32[]{:S(2)}) collective-permute-start(f32[16,512]{1,0:T(8,128)S(1)} %get-tuple-element.30), channel_id=1, source_target_pairs={{0,8},{2,10},{8,0},{10,2},{16,24},{18,26},{24,16},{26,18},{1,9},{3... | collective-permute-start | bytes 98312 | tf_op jit(solution)/shard_map/ppermute | solution.py:278
  123.6 7.8 %collective-permute-start.8 = (f32[16,512]{1,0:T(8,128)S(1)}, f32[16,512]{1,0:T(8,128)S(1)}, u32[]{:S(2)}, u32[]{:S(2)}) collective-permute-start(f32[16,512]{1,0:T(8,128)S(1)} %get-tuple-element.31), channel_id=1, source_target_pairs={{0,10},{2,8},{8,2},{10,0},{16,26},{18,24},{24,18},{26,16},{1,11},{... | collective-permute-start | bytes 98312 | tf_op jit(solution)/shard_map/ppermute | solution.py:278
  123.8 7.6 %collective-permute-start.9 = (f32[16,512]{1,0:T(8,128)S(1)}, f32[16,512]{1,0:T(8,128)S(1)}, u32[]{:S(2)}, u32[]{:S(2)}) collective-permute-start(f32[16,512]{1,0:T(8,128)S(1)} %get-tuple-element.32), channel_id=1, source_target_pairs={{0,16},{2,18},{8,24},{10,26},{16,0},{18,2},{24,8},{26,10},{1,17},{... | collective-permute-start | bytes 98312 | tf_op jit(solution)/shard_map/ppermute | solution.py:278

commit v3 on v2

--- a/solution.py
+++ b/solution.py
@@ -115,22 +115,22 @@
             up_t[columns, :] = up[:, columns].T
 
     grad = dot(w_out[...], up_t[...], ((1,), (0,)))
-    z0 = lax.rem(step // 2, 2)
-    for core in range(2):
-        columns = slice(core * HD, (core + 1) * HD)
-        packed[core, :, :HD] = queries[:, columns]
-        packed[core, :, HD : 2 * HD] = keys[:, columns]
-        packed[core, :, 2 * HD : 3 * HD] = values[:, columns]
-        packed[core, :, 3 * HD : 4 * HD] = grad[columns].T.astype(jnp.bfloat16)
+    z0 = lax.rem(step, 2)
+    for h in range(packed.shape[0]):
+        columns = slice(h * HD, (h + 1) * HD)
+        packed[h, :, :HD] = queries[:, columns]
+        packed[h, :, HD : 2 * HD] = keys[:, columns]
+        packed[h, :, 2 * HD : 3 * HD] = values[:, columns]
+        packed[h, :, 3 * HD : 4 * HD] = grad[columns].T.astype(jnp.bfloat16)
         for granule in range(up.shape[1] // 64):
-            start = pl.multiple_of(granule // 2 * 128 + z0 * 64 + granule % 2 * 32 + core * 16, 16)
+            start = pl.multiple_of(granule // 2 * 128 + z0 * 64 + granule % 2 * 32 + h % 2 * 16, 16)
             chunk, row = granule // 8, granule % 8 * 16
-            packed[core, row : row + 16, (chunk + 4) * HD : (chunk + 5) * HD] = up_t[pl.ds(start, 16), :]
+            packed[h, row : row + 16, (chunk + 4) * HD : (chunk + 5) * HD] = up_t[pl.ds(start, 16), :]
 
 
 def pack(rows, up, w_out):
     tokens, width = up.shape
-    step = 2 * HD
+    step = 4 * HD
     steps = width // step
     return pl.pallas_call(
         pack_kernel,
@@ -143,9 +143,9 @@
             pl.BlockSpec((tokens, step), lambda i: (0, steps + i)),
             pl.BlockSpec((tokens, step), lambda i: (0, 2 * steps + i)),
         ],
-        out_specs=pl.BlockSpec((2, tokens, 8 * HD), lambda i: (i, 0, 0)),
+        out_specs=pl.BlockSpec((step // HD, tokens, 8 * HD), lambda i: (i, 0, 0)),
         scratch_shapes=[pltpu.VMEM((width, tokens), jnp.bfloat16)],
-        compiler_params=pltpu.CompilerParams(vmem_limit_bytes=VMEM_LIMIT),
+        compiler_params=pltpu.CompilerParams(vmem_limit_bytes=60 * 1024 * 1024),
         cost_estimate=pl.CostEstimate(
             flops=2 * tokens * width * width, bytes_accessed=2 * width * width, transcendentals=0
         ),
@@ -276,10 +276,11 @@
         scratch=[pltpu.VMEM((width // 16, 4 * HD), jnp.float32)],
     )
     parts = [parts[0]] + [lax.ppermute(parts[far], eight, [(i, i ^ far) for i in range(8)]) for far in range(1, 8)]
+    d_rows = whole_call(unpack_heads_kernel, shape(rows.shape, jnp.bfloat16), "unpack_heads", d_rows)
+    parts, d_rows = lax.optimization_barrier((parts, d_rows))
     grad_w_out = whole_call(
         combine_kernel, shape((column_width, width), jnp.float32), "combine", *parts, place=place
     )
-    d_rows = whole_call(unpack_heads_kernel, shape(rows.shape, jnp.bfloat16), "unpack_heads", d_rows)
     return d_rows[None], grad_w_out.T
 
 

time: 135 us -> 129 us (0.956)
  local copies, waits for them, and re-layouts: 2.45 us -> 0.01 us
  waiting for transfers between devices: 13.7 us -> 12.1 us
    unnamed x6 -> x2, local copies, waits for them, and re-layouts: 2.45 us -> 0.01 us
    ppermute x7, waiting for transfers between devices: 6.36 us -> 4.76 us  [on_device(): lax.ppermute(parts[far], eight, [(i, i ^ far) for i in range(8)])]
  transfers between devices with their start and end apart: 14 -> 14, of which waited for: 6 -> 5; matrix products, arithmetic and copies ran while one was open for 0% -> 0% of each run, Pallas kernels for 13% -> 14%
where the time goes in v3:
time: 129 us
  blocking collectives  59.8 us (46%)
  Pallas kernels  32.3 us (25%)
  starting transfers between devices  24.1 us (19%)
  waiting for transfers between devices  12.1 us (9%)
    all_to_all x1, blocking collectives, on_device(): packed = lax.all_to_all(pack(rows, up, w_out), SEQ, 0, 0, tiled=True)  59.8 us
    pallas_call x6, Pallas kernels, whole_call(): pl.pallas_call(kernel, grid=(1,), out_shape=out, in_specs=[pl.BlockSpec(m...  24 us
    ppermute x7, starting transfers between devices, on_device(): lax.ppermute(parts[far], eight, [(i, i ^ far) for i in range(8)])  14.1 us
    pallas_call x1, Pallas kernels, pack(): pl.pallas_call(pack_kernel, grid=(steps,), out_shape=jax.ShapeDtypeStruct...  8.31 us
    ppermute x3, starting transfers between devices, on_device(): lax.ppermute(tiles[far], 'x', [(i, (i + far) % 4) for i in range(4)])  5.73 us
    ppermute x3, waiting for transfers between devices, on_device(): lax.ppermute(tiles[far], 'x', [(i, (i + far) % 4) for i in range(4)])  4.97 us
    ppermute x7, waiting for transfers between devices, on_device(): lax.ppermute(parts[far], eight, [(i, i ^ far) for i in range(8)])  4.76 us
    all_to_all x1, starting transfers between devices, on_device(): d_rows = lax.all_to_all(d_qkv, SEQ, 0, 0, tiled=True)  3.71 us
  transfers between devices with their start and end apart: 14, of which 5 were waited for; matrix products, arithmetic and copies ran while one was open for 0% of the time, Pallas kernels for 14%

profile of v3, /device:TPU:0, one launch (start us, length us, event | category | flops | bytes accessed | tf_op | source)
XLA Modules:
  0.0 129.1 jit_solution(2054214057960749269)
XLA Ops:
  0.6 8.3 %pack.1 = bf16[16,128,1024]{2,1,0:T(8,128)(2,1)} custom-call(bf16[128,2048]{1,0:T(8,128)(2,1)} %bitcast.12, bf16[2048,2048]{1,0:T(8,128)(2,1)} %w_out.1, bf16[128,6144]{1,0:T(8,128)(2,1)} %bitcast.8, bf16[128,6144]{1,0:T(8,128)(2,1)} %bitcast.9, bf16[128,6144]{1,0:T(8,128)(2,1)} %bitcast.10), custom_call_target="tpu_custom_call" | custom-call | flops 1073741824 | bytes 8388608 | tf_op jit(solution)/shard_map/pack/pallas_call | solution.py:135
  8.9 59.8 %all_to_all.10.qkv.columns = bf16[16,128,1024]{2,1,0:T(8,128)(2,1)S(1)} all-to-all(bf16[16,128,1024]{2,1,0:T(8,128)(2,1)} %pack.1), channel_id=1, replica_groups=mesh['x'=4,'ylo'=2,'z1'=2,'z0'=2,'yh'=2,'core'=2] {'z1','z0','yh','core'}, dimensions={0} | all-to-all | bytes 8388608 | tf_op jit(solution)/shard_map/all_to_all | solution.py:222
  68.7 0.0 copy-start
  68.7 5.2 %forward.1 = (bf16[16,128,128]{2,1,0:T(8,128)(2,1)S(1)}, f32[16,2,128]{2,1,0:T(2,128)S(1)}) custom-call(bf16[16,128,1024]{2,1,0:T(8,128)(2,1)S(1)} %all_to_all.10.qkv.columns), custom_call_target="tpu_custom_call" | custom-call | flops 2000000000 | bytes 4734976 | tf_op jit(solution)/shard_map/forward/pallas_call | solution.py:94
  73.9 0.1 collective-permute-start
  74.0 0.3 collective-permute-start.1
  74.3 0.0 copy-done
  74.3 12.3 %backward.1 = bf16[16,128,384]{2,1,0:T(8,128)(2,1)} custom-call(bf16[16,128,1024]{2,1,0:T(8,128)(2,1)S(1)} %all_to_all.10.qkv.columns, f32[16,2,128]{2,1,0:T(2,128)S(1)} %get-tuple-element.29.stats), custom_call_target="tpu_custom_call" | custom-call | flops 4000000000 | bytes 5783552 | tf_op jit(solution)/shard_map/backward/pallas_call | solution.py:94
  86.6 0.6 collective-permute-done.over_z
  87.2 0.0 collective-permute-done.1.over_core
  87.2 3.7 %all-to-all-start.1 = ((bf16[16,128,384]{2,1,0:T(8,128)(2,1)}), bf16[16,128,384]{2,1,0:T(8,128)(2,1)S(1)}, u32[]{:S(2)}, u32[]{:S(2)}) async-start(bf16[16,128,384]{2,1,0:T(8,128)(2,1)} %backward.1), calls=%async_computation.1 | async-start | bytes 3145728 | tf_op jit(solution)/shard_map/all_to_all | solution.py:251
  90.9 0.3 collective-permute-start.2
  91.2 0.1 pad_add_fusion.place
  91.3 1.8 %collective-permute-done.2.over_both = bf16[16,128,128]{2,1,0:T(8,128)(2,1)} collective-permute-done((bf16[16,128,128]{2,1,0:T(8,128)(2,1)S(1)}, bf16[16,128,128]{2,1,0:T(8,128)(2,1)}, u32[]{:S(2)}, u32[]{:S(2)}) %collective-permute-start.2) | collective-permute-done | bytes 524320 | tf_op jit(solution)/shard_map/ppermute | solution.py:250
  93.0 3.1 %tile.1 = (bf16[128,512]{1,0:T(8,128)(2,1)S(1)}, bf16[128,512]{1,0:T(8,128)(2,1)S(1)}, bf16[128,512]{1,0:T(8,128)(2,1)S(1)}, bf16[128,512]{1,0:T(8,128)(2,1)S(1)}) custom-call(s32[4]{0:T(128)S(1)} %pad_add_fusion.place, bf16[16,128,1024]{2,1,0:T(8,128)(2,1)} %copy-done, bf16[16,128,128]{2,1,0:T(8,128)(2,1)S(1)} %get-tuple-element.28.own, ...), custom_call_target="tpu_custom_call" | custom-call | flops 1073741824 | bytes 6815744 | tf_op jit(solution)/shard_map/tile/pallas_call | solution.py:94
  96.1 1.6 %collective-permute-start.3 = (bf16[128,512]{1,0:T(8,128)(2,1)S(1)}, bf16[128,512]{1,0:T(8,128)(2,1)S(1)}, u32[]{:S(2)}, u32[]{:S(2)}) collective-permute-start(bf16[128,512]{1,0:T(8,128)(2,1)S(1)} %get-tuple-element.33), channel_id=1, source_target_pairs={{0,32},{32,64},{64,96},{96,0},{1,33},{33,65},{65,97},{97,1},{2,34}... | collective-permute-start | bytes 393224 | tf_op jit(solution)/shard_map/ppermute | solution.py:268
  97.7 2.7 %collective-permute-start.4 = (bf16[128,512]{1,0:T(8,128)(2,1)S(1)}, bf16[128,512]{1,0:T(8,128)(2,1)S(1)}, u32[]{:S(2)}, u32[]{:S(2)}) collective-permute-start(bf16[128,512]{1,0:T(8,128)(2,1)S(1)} %get-tuple-element.34), channel_id=1, source_target_pairs={{0,64},{32,96},{64,0},{96,32},{1,65},{33,97},{65,1},{97,33},{2,66}... | collective-permute-start | bytes 393224 | tf_op jit(solution)/shard_map/ppermute | solution.py:268
  100.4 1.4 %collective-permute-start.5 = (bf16[128,512]{1,0:T(8,128)(2,1)S(1)}, bf16[128,512]{1,0:T(8,128)(2,1)S(1)}, u32[]{:S(2)}, u32[]{:S(2)}) collective-permute-start(bf16[128,512]{1,0:T(8,128)(2,1)S(1)} %get-tuple-element.35), channel_id=1, source_target_pairs={{0,96},{32,0},{64,32},{96,64},{1,97},{33,1},{65,33},{97,65},{2,98}... | collective-permute-start | bytes 393224 | tf_op jit(solution)/shard_map/ppermute | solution.py:268
  101.8 1.2 collective-permute-done.3.refs_1_
  103.0 3.8 %collective-permute-done.4.refs_2_ = bf16[128,512]{1,0:T(8,128)(2,1)S(1)} collective-permute-done((bf16[128,512]{1,0:T(8,128)(2,1)S(1)}, bf16[128,512]{1,0:T(8,128)(2,1)S(1)}, u32[]{:S(2)}, u32[]{:S(2)}) %collective-permute-start.4) | collective-permute-done | bytes 131104 | tf_op jit(solution)/shard_map/ppermute | solution.py:268
  106.8 0.0 collective-permute-done.5.refs_3_
  106.8 0.6 sum_tiles.1
  107.5 3.1 %collective-permute-start.10 = (f32[16,512]{1,0:T(8,128)S(1)}, f32[16,512]{1,0:T(8,128)S(1)}, u32[]{:S(2)}, u32[]{:S(2)}) collective-permute-start(f32[16,512]{1,0:T(8,128)S(1)} %get-tuple-element.41), channel_id=1, source_target_pairs={{0,18},{2,16},{8,26},{10,24},{16,2},{18,0},{24,10},{26,8},{1,19},{... | collective-permute-start | bytes 98312 | tf_op jit(solution)/shard_map/ppermute | solution.py:278
  110.5 2.6 %collective-permute-start.11 = (f32[16,512]{1,0:T(8,128)S(1)}, f32[16,512]{1,0:T(8,128)S(1)}, u32[]{:S(2)}, u32[]{:S(2)}) collective-permute-start(f32[16,512]{1,0:T(8,128)S(1)} %get-tuple-element.42), channel_id=1, source_target_pairs={{0,24},{2,26},{8,16},{10,18},{16,8},{18,10},{24,0},{26,2},{1,25},{... | collective-permute-start | bytes 98312 | tf_op jit(solution)/shard_map/ppermute | solution.py:278
  113.1 0.6 collective-permute-start.12
  113.8 3.3 %collective-permute-start.6 = (f32[16,512]{1,0:T(8,128)S(1)}, f32[16,512]{1,0:T(8,128)S(1)}, u32[]{:S(2)}, u32[]{:S(2)}) collective-permute-start(f32[16,512]{1,0:T(8,128)S(1)} %get-tuple-element.37), channel_id=1, source_target_pairs={{0,2},{2,0},{8,10},{10,8},{16,18},{18,16},{24,26},{26,24},{1,3},{3... | collective-permute-start | bytes 98312 | tf_op jit(solution)/shard_map/ppermute | solution.py:278
  117.0 3.0 %collective-permute-start.7 = (f32[16,512]{1,0:T(8,128)S(1)}, f32[16,512]{1,0:T(8,128)S(1)}, u32[]{:S(2)}, u32[]{:S(2)}) collective-permute-start(f32[16,512]{1,0:T(8,128)S(1)} %get-tuple-element.38), channel_id=1, source_target_pairs={{0,8},{2,10},{8,0},{10,2},{16,24},{18,26},{24,16},{26,18},{1,9},{3... | collective-permute-start | bytes 98312 | tf_op jit(solution)/shard_map/ppermute | solution.py:278
  120.1 0.0 collective-permute-done.10.refs_5_
  120.1 0.2 collective-permute-start.8
  120.3 0.0 collective-permute-done.11.refs_6_
  120.3 1.3 collective-permute-start.9
  121.5 0.0 all-to-all-done.1.packed
  121.5 1.6 %unpack_heads.1 = bf16[128,6144]{1,0:T(8,128)(2,1)} custom-call(bf16[16,128,384]{2,1,0:T(8,128)(2,1)S(1)} %all-to-all-done.1.packed), custom_call_target="tpu_custom_call" | custom-call | bytes 3145728 | tf_op jit(solution)/shard_map/unpack_heads/pallas_call | solution.py:94
  123.1 0.0 collective-permute-done.12.refs_7_
  123.1 0.0 collective-permute-done.6.refs_1_
  123.1 0.0 collective-permute-done.7.refs_2_
  123.1 4.7 %collective-permute-done.8.refs_3_ = f32[16,512]{1,0:T(8,128)S(1)} collective-permute-done((f32[16,512]{1,0:T(8,128)S(1)}, f32[16,512]{1,0:T(8,128)S(1)}, u32[]{:S(2)}, u32[]{:S(2)}) %collective-permute-start.8) | collective-permute-done | bytes 32800 | tf_op jit(solution)/shard_map/ppermute | solution.py:278
  127.9 0.0 collective-permute-done.9.refs_4_
  127.9 1.3 combine.1
Async XLA Ops:
  68.7 5.6 %copy-start = (bf16[16,128,1024]{2,1,0:T(8,128)(2,1)}, bf16[16,128,1024]{2,1,0:T(8,128)(2,1)S(1)}, u32[]{:S(2)}) copy-start(bf16[16,128,1024]{2,1,0:T(8,128)(2,1)S(1)} %all_to_all.10.qkv.columns) | copy-start | bytes 12582916
  73.9 13.3 %collective-permute-start = (bf16[16,128,128]{2,1,0:T(8,128)(2,1)S(1)}, bf16[16,128,128]{2,1,0:T(8,128)(2,1)S(1)}, u32[]{:S(2)}, u32[]{:S(2)}) collective-permute-start(bf16[16,128,128]{2,1,0:T(8,128)(2,1)S(1)} %get-tuple-element.28.own), channel_id=1, source_target_pairs={{0,4},{4,0},{1,5},{5,1},{2,6},{6,2},{3,7},{7,3},{8,12},{12,8},{9,1... | collective-permute-start | bytes 1572872 | tf_op jit(solution)/shard_map/ppermute | solution.py:233
  74.0 13.2 %collective-permute-start.1 = (bf16[16,128,128]{2,1,0:T(8,128)(2,1)S(1)}, bf16[16,128,128]{2,1,0:T(8,128)(2,1)S(1)}, u32[]{:S(2)}, u32[]{:S(2)}) collective-permute-start(bf16[16,128,128]{2,1,0:T(8,128)(2,1)S(1)} %get-tuple-element.28.own), channel_id=1, source_target_pairs={{0,1},{1,0},{2,3},{3,2},{4,5},{5,4},{6,7},{7,6},{8,9},{9,8},{10,11... | collective-permute-start | bytes 1572872 | tf_op jit(solution)/shard_map/ppermute | solution.py:234
  87.2 34.3 %all-to-all-start.1 = ((bf16[16,128,384]{2,1,0:T(8,128)(2,1)}), bf16[16,128,384]{2,1,0:T(8,128)(2,1)S(1)}, u32[]{:S(2)}, u32[]{:S(2)}) async-start(bf16[16,128,384]{2,1,0:T(8,128)(2,1)} %backward.1), calls=%async_computation.1 | async-start | bytes 3145728 | tf_op jit(solution)/shard_map/all_to_all | solution.py:251
  90.9 2.1 %collective-permute-start.2 = (bf16[16,128,128]{2,1,0:T(8,128)(2,1)S(1)}, bf16[16,128,128]{2,1,0:T(8,128)(2,1)}, u32[]{:S(2)}, u32[]{:S(2)}) collective-permute-start(bf16[16,128,128]{2,1,0:T(8,128)(2,1)S(1)} %collective-permute-done.over_z), channel_id=1, source_target_pairs={{0,1},{1,0},{2,3},{3,2},{4,5},{5,4},{6,7},{7,6},{8,9},{9,8},{10,11... | collective-permute-start | bytes 1572872 | tf_op jit(solution)/shard_map/ppermute | solution.py:250
  96.1 6.9 %collective-permute-start.3 = (bf16[128,512]{1,0:T(8,128)(2,1)S(1)}, bf16[128,512]{1,0:T(8,128)(2,1)S(1)}, u32[]{:S(2)}, u32[]{:S(2)}) collective-permute-start(bf16[128,512]{1,0:T(8,128)(2,1)S(1)} %get-tuple-element.33), channel_id=1, source_target_pairs={{0,32},{32,64},{64,96},{96,0},{1,33},{33,65},{65,97},{97,1},{2,34}... | collective-permute-start | bytes 393224 | tf_op jit(solution)/shard_map/ppermute | solution.py:268
  97.7 9.1 %collective-permute-start.4 = (bf16[128,512]{1,0:T(8,128)(2,1)S(1)}, bf16[128,512]{1,0:T(8,128)(2,1)S(1)}, u32[]{:S(2)}, u32[]{:S(2)}) collective-permute-start(bf16[128,512]{1,0:T(8,128)(2,1)S(1)} %get-tuple-element.34), channel_id=1, source_target_pairs={{0,64},{32,96},{64,0},{96,32},{1,65},{33,97},{65,1},{97,33},{2,66}... | collective-permute-start | bytes 393224 | tf_op jit(solution)/shard_map/ppermute | solution.py:268
  100.4 6.4 %collective-permute-start.5 = (bf16[128,512]{1,0:T(8,128)(2,1)S(1)}, bf16[128,512]{1,0:T(8,128)(2,1)S(1)}, u32[]{:S(2)}, u32[]{:S(2)}) collective-permute-start(bf16[128,512]{1,0:T(8,128)(2,1)S(1)} %get-tuple-element.35), channel_id=1, source_target_pairs={{0,96},{32,0},{64,32},{96,64},{1,97},{33,1},{65,33},{97,65},{2,98}... | collective-permute-start | bytes 393224 | tf_op jit(solution)/shard_map/ppermute | solution.py:268
  107.5 12.6 %collective-permute-start.10 = (f32[16,512]{1,0:T(8,128)S(1)}, f32[16,512]{1,0:T(8,128)S(1)}, u32[]{:S(2)}, u32[]{:S(2)}) collective-permute-start(f32[16,512]{1,0:T(8,128)S(1)} %get-tuple-element.41), channel_id=1, source_target_pairs={{0,18},{2,16},{8,26},{10,24},{16,2},{18,0},{24,10},{26,8},{1,19},{... | collective-permute-start | bytes 98312 | tf_op jit(solution)/shard_map/ppermute | solution.py:278
  110.5 9.7 %collective-permute-start.11 = (f32[16,512]{1,0:T(8,128)S(1)}, f32[16,512]{1,0:T(8,128)S(1)}, u32[]{:S(2)}, u32[]{:S(2)}) collective-permute-start(f32[16,512]{1,0:T(8,128)S(1)} %get-tuple-element.42), channel_id=1, source_target_pairs={{0,24},{2,26},{8,16},{10,18},{16,8},{18,10},{24,0},{26,2},{1,25},{... | collective-permute-start | bytes 98312 | tf_op jit(solution)/shard_map/ppermute | solution.py:278
  113.1 10.0 %collective-permute-start.12 = (f32[16,512]{1,0:T(8,128)S(1)}, f32[16,512]{1,0:T(8,128)S(1)}, u32[]{:S(2)}, u32[]{:S(2)}) collective-permute-start(f32[16,512]{1,0:T(8,128)S(1)} %get-tuple-element.43), channel_id=1, source_target_pairs={{0,26},{2,24},{8,18},{10,16},{16,10},{18,8},{24,2},{26,0},{1,27},{... | collective-permute-start | bytes 98312 | tf_op jit(solution)/shard_map/ppermute | solution.py:278
  113.8 9.4 %collective-permute-start.6 = (f32[16,512]{1,0:T(8,128)S(1)}, f32[16,512]{1,0:T(8,128)S(1)}, u32[]{:S(2)}, u32[]{:S(2)}) collective-permute-start(f32[16,512]{1,0:T(8,128)S(1)} %get-tuple-element.37), channel_id=1, source_target_pairs={{0,2},{2,0},{8,10},{10,8},{16,18},{18,16},{24,26},{26,24},{1,3},{3... | collective-permute-start | bytes 98312 | tf_op jit(solution)/shard_map/ppermute | solution.py:278
  117.0 6.1 %collective-permute-start.7 = (f32[16,512]{1,0:T(8,128)S(1)}, f32[16,512]{1,0:T(8,128)S(1)}, u32[]{:S(2)}, u32[]{:S(2)}) collective-permute-start(f32[16,512]{1,0:T(8,128)S(1)} %get-tuple-element.38), channel_id=1, source_target_pairs={{0,8},{2,10},{8,0},{10,2},{16,24},{18,26},{24,16},{26,18},{1,9},{3... | collective-permute-start | bytes 98312 | tf_op jit(solution)/shard_map/ppermute | solution.py:278
  120.1 7.8 %collective-permute-start.8 = (f32[16,512]{1,0:T(8,128)S(1)}, f32[16,512]{1,0:T(8,128)S(1)}, u32[]{:S(2)}, u32[]{:S(2)}) collective-permute-start(f32[16,512]{1,0:T(8,128)S(1)} %get-tuple-element.39), channel_id=1, source_target_pairs={{0,10},{2,8},{8,2},{10,0},{16,26},{18,24},{24,18},{26,16},{1,11},{... | collective-permute-start | bytes 98312 | tf_op jit(solution)/shard_map/ppermute | solution.py:278
  120.3 7.6 %collective-permute-start.9 = (f32[16,512]{1,0:T(8,128)S(1)}, f32[16,512]{1,0:T(8,128)S(1)}, u32[]{:S(2)}, u32[]{:S(2)}) collective-permute-start(f32[16,512]{1,0:T(8,128)S(1)} %get-tuple-element.40), channel_id=1, source_target_pairs={{0,16},{2,18},{8,24},{10,26},{16,0},{18,2},{24,8},{26,10},{1,17},{... | collective-permute-start | bytes 98312 | tf_op jit(solution)/shard_map/ppermute | solution.py:278

commit v4 on v3

--- a/solution.py
+++ b/solution.py
@@ -43,7 +43,18 @@
     return jnp.concatenate([turned[:, c * BLOCK : (c + 1) * BLOCK] for c in seen], axis=1)
 
 
-def forward_kernel(qkv, attended, stats, values_t):
+def halves(first, second):
+    first, second = first.astype(jnp.float32), second.astype(jnp.float32)
+    half = HD // 2
+    return (
+        jnp.concatenate([first[:, :half], second[:, :half]], axis=1),
+        jnp.concatenate([first[:, half:], second[:, half:]], axis=1),
+    )
+
+
+def forward_kernel(place, qkv, near, far, stats, values_t):
+    even = None
+    first = place[3] // 2 % 2 == 0
     for c in range(NB):
         values_t[:, c * BLOCK : (c + 1) * BLOCK] = qkv[c, :, 2 * HD :].T
     for b in range(NB):
@@ -52,7 +63,13 @@
         weights = jnp.exp2((scores - row_max) * EXP_SCALE)
         inverse = 1.0 / jnp.sum(weights, axis=0, keepdims=True)
         att = dot(transposed(values_t, seen), weights.astype(jnp.bfloat16), ((1,), (0,)))
-        attended[b] = (att * inverse).astype(jnp.bfloat16)
+        att = att * inverse
+        if b % 2 == 0:
+            even = att
+        else:
+            low, high = halves(even, att)
+            near[b // 2] = jnp.where(first, low, high).astype(jnp.bfloat16)
+            far[b // 2] = jnp.where(first, high, low).astype(jnp.bfloat16)
         stats[b] = jnp.concatenate([row_max, inverse], axis=0)
 
 
@@ -115,17 +132,25 @@
             up_t[columns, :] = up[:, columns].T
 
     grad = dot(w_out[...], up_t[...], ((1,), (0,)))
-    z0 = lax.rem(step, 2)
+    z1, z0 = step // 2, lax.rem(step, 2)
     for h in range(packed.shape[0]):
         columns = slice(h * HD, (h + 1) * HD)
         packed[h, :, :HD] = queries[:, columns]
         packed[h, :, HD : 2 * HD] = keys[:, columns]
         packed[h, :, 2 * HD : 3 * HD] = values[:, columns]
         packed[h, :, 3 * HD : 4 * HD] = grad[columns].T.astype(jnp.bfloat16)
-        for granule in range(up.shape[1] // 64):
-            start = pl.multiple_of(granule // 2 * 128 + z0 * 64 + granule % 2 * 32 + h % 2 * 16, 16)
-            chunk, row = granule // 8, granule % 8 * 16
-            packed[h, row : row + 16, (chunk + 4) * HD : (chunk + 5) * HD] = up_t[pl.ds(start, 16), :]
+    for core in range(2):
+        chunks = []
+        for chunk in range(4):
+            starts = [
+                chunk * 512 + n // 4 * 256 + z1 * 128 + n // 2 % 2 * 64 + n % 2 * 32 + core * 16 for n in range(8)
+            ]
+            chunks.append(jnp.concatenate([up_t[pl.ds(pl.multiple_of(n, 16), 16), :] for n in starts], axis=0))
+        for side in range(2):
+            low, high = halves(chunks[2 * side], chunks[2 * side + 1])
+            piece = jnp.where(z0 == 0, low, high).astype(jnp.bfloat16)
+            for h in (core, core + 2):
+                packed[h, :, (side + 4) * HD : (side + 5) * HD] = piece
 
 
 def pack(rows, up, w_out):
@@ -135,7 +160,7 @@
     return pl.pallas_call(
         pack_kernel,
         grid=(steps,),
-        out_shape=jax.ShapeDtypeStruct((width // HD, tokens, 8 * HD), jnp.bfloat16),
+        out_shape=jax.ShapeDtypeStruct((width // HD, tokens, 6 * HD), jnp.bfloat16),
         in_specs=[
             pl.BlockSpec((tokens, width), lambda i: (0, 0)),
             pl.BlockSpec((step, width), lambda i: (i, 0)),
@@ -143,7 +168,7 @@
             pl.BlockSpec((tokens, step), lambda i: (0, steps + i)),
             pl.BlockSpec((tokens, step), lambda i: (0, 2 * steps + i)),
         ],
-        out_specs=pl.BlockSpec((step // HD, tokens, 8 * HD), lambda i: (i, 0, 0)),
+        out_specs=pl.BlockSpec((step // HD, tokens, 6 * HD), lambda i: (i, 0, 0)),
         scratch_shapes=[pltpu.VMEM((width, tokens), jnp.bfloat16)],
         compiler_params=pltpu.CompilerParams(vmem_limit_bytes=60 * 1024 * 1024),
         cost_estimate=pl.CostEstimate(
@@ -161,18 +186,17 @@
             rows[:, column : column + HD] = packed[h, :, kind * HD : (kind + 1) * HD]
 
 
-def tile_kernel(factor, place, columns, own, over_core, over_z, over_both, *outs):
-    *outs, product = outs
-    blocks = range(NB)
-    lhs = jnp.concatenate(
-        [
-            jnp.concatenate([columns[b, :, chunk * HD : (chunk + 1) * HD] for b in blocks], axis=1)
-            for chunk in range(4)
-        ],
-        axis=0,
-    )
+def tile_kernel(factor, place, columns, *refs):
+    parts, outs, product = refs[:8], refs[8:-1], refs[-1]
+    lhs = []
+    for side in range(2):
+        lanes = slice(side * HD, (side + 1) * HD)
+        pairs = [halves(columns[2 * m, :, lanes], columns[2 * m + 1, :, lanes]) for m in range(NB // 2)]
+        for half in range(2):
+            lhs.append(jnp.concatenate([p[half].astype(jnp.bfloat16) for p in pairs], axis=1))
+    lhs = jnp.concatenate(lhs, axis=0)
     rhs = jnp.concatenate(
-        [jnp.concatenate([part[b] for b in blocks], axis=1) for part in (own, over_core, over_z, over_both)],
+        [jnp.concatenate([part[m] for m in range(NB // 2)], axis=1) for part in parts],
         axis=0,
     )
     product[...] = dot(lhs, rhs, ((1,), (1,))) * factor
@@ -182,28 +206,29 @@
         out[...] = product[pl.ds(pl.multiple_of(to * rows, rows), rows), :].astype(out.dtype)
 
 
-def sum_kernel(place, *refs):
-    tiles, outs, total = refs[:4], refs[4:-1], refs[-1]
+def sum_kernel(*refs):
+    *tiles, out = refs
     value = tiles[0][...].astype(jnp.float32)
     for tile in tiles[1:]:
         value += tile[...].astype(jnp.float32)
-    total[...] = value
-    rows = outs[0].shape[0]
-    for far, out in enumerate(outs):
-        to = place[3] ^ far
-        out[...] = total[pl.ds(pl.multiple_of(to * rows, rows), rows), :]
-
-
-def combine_kernel(place, *refs):
-    *parts, out = refs
-    for far in range(4):
-        source = place[3] ^ far
-        z1, yh = lax.rem(source // 2, 2), lax.rem(source, 2)
-        total = parts[far][...] + parts[far + 4][...]
-        for near in range(4):
-            head = z1 * 8 + (place[0] ^ (near // 2)) * 4 + yh * 2 + (place[1] ^ (near % 2))
-            start = pl.multiple_of(head * HD, HD)
-            out[:, pl.ds(start, HD)] = total[:, near * HD : (near + 1) * HD]
+    rows = out.shape[1]
+    for to in range(out.shape[0]):
+        out[to] = value[to * rows : (to + 1) * rows].astype(out.dtype)
+
+
+def combine_kernel(place, parts, out):
+    for yh in range(2):
+        for head_z0 in range(2):
+            for far in range(4):
+                far_z1, far_core = far // 2, far % 2
+                total = None
+                for ylo in range(2):
+                    for sender_z0 in range(2):
+                        lane = ((head_z0 ^ sender_z0) * 4 + far_z1 * 2 + far_core) * HD
+                        piece = parts[ylo * 4 + sender_z0 * 2 + yh, :, lane : lane + HD].astype(jnp.float32)
+                        total = piece if total is None else total + piece
+                head = (place[0] ^ far_z1) * 8 + head_z0 * 4 + yh * 2 + (place[1] ^ far_core)
+                out[:, pl.ds(pl.multiple_of(head * HD, HD), HD)] = total
 
 
 def on_device(projected, upstream, w_out, partners):
@@ -216,22 +241,27 @@
     column_width = width // (dp * heads)
     factor = (tokens * heads * dp) ** (-0.5)
     shape = jax.ShapeDtypeStruct
-    eight = ("ylo", "z1", "yh")
-    place = jnp.stack([lax.axis_index(a) for a in ("z0", "core", "x", eight)]).astype(jnp.int32)
+    eight = ("ylo", "z0", "yh")
+    place = jnp.stack([lax.axis_index(a) for a in ("z1", "core", "x", eight)]).astype(jnp.int32)
 
     packed = lax.all_to_all(pack(rows, up, w_out), SEQ, 0, 0, tiled=True)
-    attended, stats = whole_call(
+    near, far, stats = whole_call(
         forward_kernel,
-        (shape((NB, HD, BLOCK), jnp.bfloat16), shape((NB, 2, BLOCK), jnp.float32)),
+        (shape((NB // 2, HD, BLOCK), jnp.bfloat16),) * 2 + (shape((NB, 2, BLOCK), jnp.float32),),
         "forward",
         packed,
+        place=place,
         blocks={0: ((NB, BLOCK, 3 * HD), (0, 0, 0))},
         scratch=[pltpu.VMEM((HD, NB * BLOCK), jnp.bfloat16)],
         flops=2_000_000_000,
     )
     flip = [(0, 1), (1, 0)]
-    over_z = lax.ppermute(attended, "z0", flip)
-    over_core = lax.ppermute(attended, "core", flip)
+    over_z = [
+        lax.ppermute(near, "z1", flip),
+        lax.ppermute(far, "z0", flip),
+        lax.ppermute(far, ("z1", "z0"), [(i, 3 - i) for i in range(4)]),
+    ]
+    over_core = lax.ppermute(near, "core", flip)
     d_qkv = whole_call(
         backward_kernel,
         shape((NB, BLOCK, 3 * HD), jnp.bfloat16),
@@ -247,39 +277,31 @@
         flops=4_000_000_000,
     )
     d_qkv, over_z, over_core = lax.optimization_barrier((d_qkv, over_z, over_core))
-    over_both = lax.ppermute(over_z, "core", flip)
+    parts = [near, over_core]
+    for part in over_z:
+        parts += [part, lax.ppermute(part, "core", flip)]
     d_rows = lax.all_to_all(d_qkv, SEQ, 0, 0, tiled=True)
 
     tiles = whole_call(
         functools.partial(tile_kernel, factor),
-        (shape((width // 16, 4 * HD), jnp.bfloat16),) * 4,
+        (shape((width // 16, 8 * HD), jnp.bfloat16),) * 4,
         "tile",
         packed,
-        attended,
-        over_core,
-        over_z,
-        over_both,
+        *parts,
         place=place,
-        blocks={0: ((NB, BLOCK, 4 * HD), (0, 0, 1))},
-        scratch=[pltpu.VMEM((width // 4, 4 * HD), jnp.float32)],
+        blocks={0: ((NB, BLOCK, 2 * HD), (0, 0, 2))},
+        scratch=[pltpu.VMEM((width // 4, 8 * HD), jnp.float32)],
         flops=2 * (width // 4) ** 2 * heads * tokens,
     )
     tiles = [tiles[0]] + [
         lax.ppermute(tiles[far], "x", [(i, (i + far) % 4) for i in range(4)]) for far in range(1, 4)
     ]
-    parts = whole_call(
-        sum_kernel,
-        (shape((column_width, 4 * HD), jnp.float32),) * 8,
-        "sum_tiles",
-        *tiles,
-        place=place,
-        scratch=[pltpu.VMEM((width // 16, 4 * HD), jnp.float32)],
-    )
-    parts = [parts[0]] + [lax.ppermute(parts[far], eight, [(i, i ^ far) for i in range(8)]) for far in range(1, 8)]
+    parts = whole_call(sum_kernel, shape((8, column_width, 8 * HD), jnp.bfloat16), "sum_tiles", *tiles)
+    parts, d_rows = lax.optimization_barrier((parts, d_rows))
+    parts = lax.all_to_all(parts, eight, 0, 0, tiled=True)
     d_rows = whole_call(unpack_heads_kernel, shape(rows.shape, jnp.bfloat16), "unpack_heads", d_rows)
-    parts, d_rows = lax.optimization_barrier((parts, d_rows))
     grad_w_out = whole_call(
-        combine_kernel, shape((column_width, width), jnp.float32), "combine", *parts, place=place
+        combine_kernel, shape((column_width, width), jnp.float32), "combine", parts, place=place
     )
     return d_rows[None], grad_w_out.T
 

time: 129 us -> 122 us (0.946)
  blocking collectives: 59.8 us -> 0 us
  waiting for transfers between devices: 12.1 us -> 59.6 us
  starting transfers between devices: 24.1 us -> 27.4 us
  local copies, waits for them, and re-layouts: 0.01 us -> 2.6 us
    all_to_all x1 -> x0, blocking collectives: 59.8 us -> none  [on_device(): packed = lax.all_to_all(pack(rows, up, w_out), SEQ, 0, 0, tiled=True)]
    all_to_all x0 -> x2, waiting for transfers between devices: none -> 46.2 us  [the longest x1 40.5 us: on_device(): packed = lax.all_to_all(pack(rows, up, w_out), SEQ, 0, 0, tiled=True)]
    all_to_all x0 -> x2, starting transfers between devices: none -> 12.2 us  [the longest x1 8.13 us: on_device(): packed = lax.all_to_all(pack(rows, up, w_out), SEQ, 0, 0, tiled=True)]
    ppermute x10 -> x7, starting transfers between devices: 14.7 us -> 5.68 us  [the longest x1 3.18 us: on_device(): lax.ppermute(near, 'z1', flip)]
    ppermute x10 -> x7, waiting for transfers between devices: 7.14 us -> 1.47 us  [the longest x3 1.46 us: on_device(): parts += [part, lax.ppermute(part, 'core', flip)]]
    ppermute x3, waiting for transfers between devices: 4.97 us -> 10.6 us  [on_device(): lax.ppermute(tiles[far], 'x', [(i, (i + far) % 4) for i in range(4)])]
    unnamed x2 -> x16, local copies, waits for them, and re-layouts: 0.01 us -> 2.6 us
    all_to_all x1, waiting for transfers between devices: 0.01 us -> 1.3 us  [on_device(): d_rows = lax.all_to_all(d_qkv, SEQ, 0, 0, tiled=True)]
  transfers between devices with their start and end apart: 14 -> 13, of which waited for: 5 -> 8; matrix products, arithmetic and copies ran while one was open for 0% -> 0% of each run, Pallas kernels for 14% -> 13%
where the time goes in v4:
time: 122 us
  waiting for transfers between devices  59.6 us (49%)
  Pallas kernels  31.3 us (26%)
  starting transfers between devices  27.4 us (22%)
  local copies, waits for them, and re-layouts  2.6 us (2%)
    all_to_all x1, waiting for transfers between devices, on_device(): packed = lax.all_to_all(pack(rows, up, w_out), SEQ, 0, 0, tiled=True)  40.5 us
    pallas_call x6, Pallas kernels, whole_call(): pl.pallas_call(kernel, grid=(1,), out_shape=out, in_specs=[pl.BlockSpec(m...  23.6 us
    ppermute x3, waiting for transfers between devices, on_device(): lax.ppermute(tiles[far], 'x', [(i, (i + far) % 4) for i in range(4)])  10.6 us
    all_to_all x1, starting transfers between devices, on_device(): packed = lax.all_to_all(pack(rows, up, w_out), SEQ, 0, 0, tiled=True)  8.13 us
    pallas_call x1, Pallas kernels, pack(): pl.pallas_call(pack_kernel, grid=(steps,), out_shape=jax.ShapeDtypeStruct...  7.68 us
    ppermute x3, starting transfers between devices, on_device(): lax.ppermute(tiles[far], 'x', [(i, (i + far) % 4) for i in range(4)])  5.73 us
    all_to_all x1, waiting for transfers between devices, on_device(): parts = lax.all_to_all(parts, eight, 0, 0, tiled=True)  5.69 us
    all_to_all x1, starting transfers between devices, on_device(): parts = lax.all_to_all(parts, eight, 0, 0, tiled=True)  4.04 us
  transfers between devices with their start and end apart: 13, of which 8 were waited for; matrix products, arithmetic and copies ran while one was open for 0% of the time, Pallas kernels for 13%

profile of v4, /device:TPU:0, one launch (start us, length us, event | category | flops | bytes accessed | tf_op | source)
XLA Modules:
  0.0 121.7 jit_solution(17974653641932002480)
XLA Ops:
  0.6 7.7 %pack.1 = bf16[16,128,768]{2,1,0:T(8,128)(2,1)} custom-call(bf16[128,2048]{1,0:T(8,128)(2,1)} %bitcast.12, bf16[2048,2048]{1,0:T(8,128)(2,1)} %w_out.1, bf16[128,6144]{1,0:T(8,128)(2,1)} %bitcast.8, bf16[128,6144]{1,0:T(8,128)(2,1)} %bitcast.9, bf16[128,6144]{1,0:T(8,128)(2,1)} %bitcast.10), custom_call_target="tpu_custom_call" | custom-call | flops 1073741824 | bytes 8388608 | tf_op jit(solution)/shard_map/pack/pallas_call | solution.py:160
  8.3 8.1 %all-to-all-start = ((bf16[16,128,768]{2,1,0:T(8,128)(2,1)}), bf16[16,128,768]{2,1,0:T(8,128)(2,1)S(1)}, u32[]{:S(2)}, u32[]{:S(2)}) async-start(bf16[16,128,768]{2,1,0:T(8,128)(2,1)} %pack.1), calls=%async_computation | async-start | bytes 6291456 | tf_op jit(solution)/shard_map/all_to_all | solution.py:247
  16.5 0.1 pad_add_fusion.place
  16.5 40.5 %all-to-all-done.qkv.columns = bf16[16,128,768]{2,1,0:T(8,128)(2,1)S(1)} async-done(((bf16[16,128,768]{2,1,0:T(8,128)(2,1)}), bf16[16,128,768]{2,1,0:T(8,128)(2,1)S(1)}, u32[]{:S(2)}, u32[]{:S(2)}) %all-to-all-start) | async-done | bytes 3145760 | tf_op jit(solution)/shard_map/all_to_all | solution.py:247
  57.0 0.0 copy-start
  57.0 6.0 %forward.1 = (bf16[8,128,128]{2,1,0:T(8,128)(2,1)S(1)}, bf16[8,128,128]{2,1,0:T(8,128)(2,1)S(1)}, f32[16,2,128]{2,1,0:T(2,128)S(1)}) custom-call(s32[4]{0:T(128)S(1)} %pad_add_fusion.place, bf16[16,128,768]{2,1,0:T(8,128)(2,1)S(1)} %all-to-all-done.qkv.columns), custom_call_target="tpu_custom_call" | custom-call | flops 2000000000 | bytes 3686400 | tf_op jit(solution)/shard_map/forward/pallas_call | solution.py:111
  63.0 1.6 %collective-permute-start.2 = (bf16[8,128,128]{2,1,0:T(8,128)(2,1)S(1)}, bf16[8,128,128]{2,1,0:T(8,128)(2,1)S(1)}, u32[]{:S(2)}, u32[]{:S(2)}) collective-permute-start(bf16[8,128,128]{2,1,0:T(8,128)(2,1)S(1)} %get-tuple-element.18), channel_id=1, source_target_pairs={{0,12},{4,8},{8,4},{12,0},{1,13},{5,9},{9,5},{13,1},{2,14},{6,10},... | collective-permute-start | bytes 786440 | tf_op jit(solution)/shard_map/ppermute | solution.py:262
  64.6 0.0 collective-permute-start.1
  64.6 0.0 collective-permute-start.3
  64.6 3.2 %collective-permute-start = (bf16[8,128,128]{2,1,0:T(8,128)(2,1)S(1)}, bf16[8,128,128]{2,1,0:T(8,128)(2,1)}, u32[]{:S(2)}, u32[]{:S(2)}) collective-permute-start(bf16[8,128,128]{2,1,0:T(8,128)(2,1)S(1)} %get-tuple-element.16.refs_0_), channel_id=1, source_target_pairs={{0,8},{8,0},{1,9},{9,1},{2,10},{10,2},{3,11},{11,3},{4,12},{12,4},... | collective-permute-start | bytes 786440 | tf_op jit(solution)/shard_map/ppermute | solution.py:260
  67.8 0.0 copy-done
  67.8 11.1 %backward.1 = bf16[16,128,384]{2,1,0:T(8,128)(2,1)S(1)} custom-call(bf16[16,128,768]{2,1,0:T(8,128)(2,1)S(1)} %all-to-all-done.qkv.columns, f32[16,2,128]{2,1,0:T(2,128)S(1)} %get-tuple-element.17.stats), custom_call_target="tpu_custom_call" | custom-call | flops 4000000000 | bytes 4734976 | tf_op jit(solution)/shard_map/backward/pallas_call | solution.py:111
  79.0 0.0 copy-start.1
  79.0 1.1 copy-done.1
  80.1 0.0 collective-permute-done.2.refs_6_
  80.1 0.0 copy-start.2
  80.1 0.0 collective-permute-done.1.refs_4_
  80.1 0.0 copy-start.4
  80.1 0.0 collective-permute-done.3.refs_1_
  80.2 0.7 copy-done.2
  80.8 0.1 copy-done.4
  80.9 0.0 copy-start.6
  80.9 0.7 copy-done.6
  81.6 0.0 collective-permute-done.refs_2_
  81.6 0.0 copy-start.5
  81.6 3.9 %all-to-all-start.1 = ((bf16[16,128,384]{2,1,0:T(8,128)(2,1)}), bf16[16,128,384]{2,1,0:T(8,128)(2,1)S(1)}, u32[]{:S(2)}, u32[]{:S(2)}) async-start(bf16[16,128,384]{2,1,0:T(8,128)(2,1)} %copy-done.1), calls=%async_computation.1 | async-start | bytes 3145728 | tf_op jit(solution)/shard_map/all_to_all | solution.py:283
  85.5 0.3 collective-permute-start.4
  85.8 0.0 copy-done.5
  85.8 0.3 collective-permute-start.5
  86.1 0.0 copy-done.3
  86.1 0.3 collective-permute-start.6
  86.4 0.9 collective-permute-done.4.refs_3_
  87.3 0.2 collective-permute-done.5.refs_5_
  87.5 0.4 collective-permute-done.6.refs_7_
  87.8 0.0 copy-done.7
  87.8 2.8 %tile.1 = (bf16[128,1024]{1,0:T(8,128)(2,1)S(1)}, bf16[128,1024]{1,0:T(8,128)(2,1)S(1)}, bf16[128,1024]{1,0:T(8,128)(2,1)S(1)}, bf16[128,1024]{1,0:T(8,128)(2,1)S(1)}) custom-call(s32[4]{0:T(128)S(1)} %pad_add_fusion.place, bf16[16,128,768]{2,1,0:T(8,128)(2,1)} %copy-done, bf16[8,128,128]{2,1,0:T(8,128)(2,1)S(1)} %get-tuple-element.16.refs_0_, ...), custom_call_target="tpu_custom_call" | custom-call | flops 1073741824 | bytes 6291456 | tf_op jit(solution)/shard_map/tile/pallas_call | solution.py:111
  90.6 1.6 %collective-permute-start.7 = (bf16[128,1024]{1,0:T(8,128)(2,1)S(1)}, bf16[128,1024]{1,0:T(8,128)(2,1)S(1)}, u32[]{:S(2)}, u32[]{:S(2)}) collective-permute-start(bf16[128,1024]{1,0:T(8,128)(2,1)S(1)} %get-tuple-element.24), channel_id=1, source_target_pairs={{0,32},{32,64},{64,96},{96,0},{1,33},{33,65},{65,97},{97,1},{2,34}... | collective-permute-start | bytes 786440 | tf_op jit(solution)/shard_map/ppermute | solution.py:297
  92.2 2.7 %collective-permute-start.8 = (bf16[128,1024]{1,0:T(8,128)(2,1)S(1)}, bf16[128,1024]{1,0:T(8,128)(2,1)S(1)}, u32[]{:S(2)}, u32[]{:S(2)}) collective-permute-start(bf16[128,1024]{1,0:T(8,128)(2,1)S(1)} %get-tuple-element.25), channel_id=1, source_target_pairs={{0,64},{32,96},{64,0},{96,32},{1,65},{33,97},{65,1},{97,33},{2,66}... | collective-permute-start | bytes 786440 | tf_op jit(solution)/shard_map/ppermute | solution.py:297
  94.9 1.4 %collective-permute-start.9 = (bf16[128,1024]{1,0:T(8,128)(2,1)S(1)}, bf16[128,1024]{1,0:T(8,128)(2,1)S(1)}, u32[]{:S(2)}, u32[]{:S(2)}) collective-permute-start(bf16[128,1024]{1,0:T(8,128)(2,1)S(1)} %get-tuple-element.26), channel_id=1, source_target_pairs={{0,96},{32,0},{64,32},{96,64},{1,97},{33,1},{65,33},{97,65},{2,98}... | collective-permute-start | bytes 786440 | tf_op jit(solution)/shard_map/ppermute | solution.py:297
  96.4 4.0 %collective-permute-done.7.refs_1_ = bf16[128,1024]{1,0:T(8,128)(2,1)S(1)} collective-permute-done((bf16[128,1024]{1,0:T(8,128)(2,1)S(1)}, bf16[128,1024]{1,0:T(8,128)(2,1)S(1)}, u32[]{:S(2)}, u32[]{:S(2)}) %collective-permute-start.7) | collective-permute-done | bytes 262176 | tf_op jit(solution)/shard_map/ppermute | solution.py:297
  100.4 6.6 %collective-permute-done.8.refs_2_ = bf16[128,1024]{1,0:T(8,128)(2,1)S(1)} collective-permute-done((bf16[128,1024]{1,0:T(8,128)(2,1)S(1)}, bf16[128,1024]{1,0:T(8,128)(2,1)S(1)}, u32[]{:S(2)}, u32[]{:S(2)}) %collective-permute-start.8) | collective-permute-done | bytes 262176 | tf_op jit(solution)/shard_map/ppermute | solution.py:297
  107.0 0.0 collective-permute-done.9.refs_3_
  107.0 0.8 sum_tiles.1
  107.8 1.3 %all-to-all-done.1.packed = bf16[16,128,384]{2,1,0:T(8,128)(2,1)S(1)} async-done(((bf16[16,128,384]{2,1,0:T(8,128)(2,1)}), bf16[16,128,384]{2,1,0:T(8,128)(2,1)S(1)}, u32[]{:S(2)}, u32[]{:S(2)}) %all-to-all-start.1) | async-done | bytes 1572896 | tf_op jit(solution)/shard_map/all_to_all | solution.py:283
  109.1 4.0 %all-to-all-start.2 = ((bf16[8,16,1024]{2,1,0:T(8,128)(2,1)}), bf16[8,16,1024]{2,1,0:T(8,128)(2,1)S(1)}, u32[]{:S(2)}, u32[]{:S(2)}) async-start(bf16[8,16,1024]{2,1,0:T(8,128)(2,1)} %sum_tiles.1), calls=%async_computation.2 | async-start | bytes 524288 | tf_op jit(solution)/shard_map/all_to_all | solution.py:301
  113.2 1.6 %unpack_heads.1 = bf16[128,6144]{1,0:T(8,128)(2,1)} custom-call(bf16[16,128,384]{2,1,0:T(8,128)(2,1)S(1)} %all-to-all-done.1.packed), custom_call_target="tpu_custom_call" | custom-call | bytes 3145728 | tf_op jit(solution)/shard_map/unpack_heads/pallas_call | solution.py:111
  114.8 5.7 %all-to-all-done.2.parts = bf16[8,16,1024]{2,1,0:T(8,128)(2,1)S(1)} async-done(((bf16[8,16,1024]{2,1,0:T(8,128)(2,1)}), bf16[8,16,1024]{2,1,0:T(8,128)(2,1)S(1)}, u32[]{:S(2)}, u32[]{:S(2)}) %all-to-all-start.2) | async-done | bytes 262176 | tf_op jit(solution)/shard_map/all_to_all | solution.py:301
  120.5 1.2 %combine.1 = f32[16,2048]{1,0:T(8,128)} custom-call(s32[4]{0:T(128)S(1)} %pad_add_fusion.place, bf16[8,16,1024]{2,1,0:T(8,128)(2,1)S(1)} %all-to-all-done.2.parts), custom_call_target="tpu_custom_call" | custom-call | bytes 393216 | tf_op jit(solution)/shard_map/combine/pallas_call | solution.py:111
  (2 shorter events, 0.0 us)
Async XLA Ops:
  8.3 48.7 %all-to-all-start = ((bf16[16,128,768]{2,1,0:T(8,128)(2,1)}), bf16[16,128,768]{2,1,0:T(8,128)(2,1)S(1)}, u32[]{:S(2)}, u32[]{:S(2)}) async-start(bf16[16,128,768]{2,1,0:T(8,128)(2,1)} %pack.1), calls=%async_computation | async-start | bytes 6291456 | tf_op jit(solution)/shard_map/all_to_all | solution.py:247
  57.0 10.8 %copy-start = (bf16[16,128,768]{2,1,0:T(8,128)(2,1)}, bf16[16,128,768]{2,1,0:T(8,128)(2,1)S(1)}, u32[]{:S(2)}) copy-start(bf16[16,128,768]{2,1,0:T(8,128)(2,1)S(1)} %all-to-all-done.qkv.columns) | copy-start | bytes 9437188
  63.0 17.1 %collective-permute-start.2 = (bf16[8,128,128]{2,1,0:T(8,128)(2,1)S(1)}, bf16[8,128,128]{2,1,0:T(8,128)(2,1)S(1)}, u32[]{:S(2)}, u32[]{:S(2)}) collective-permute-start(bf16[8,128,128]{2,1,0:T(8,128)(2,1)S(1)} %get-tuple-element.18), channel_id=1, source_target_pairs={{0,12},{4,8},{8,4},{12,0},{1,13},{5,9},{9,5},{13,1},{2,14},{6,10},... | collective-permute-start | bytes 786440 | tf_op jit(solution)/shard_map/ppermute | solution.py:262
  64.6 15.5 %collective-permute-start.1 = (bf16[8,128,128]{2,1,0:T(8,128)(2,1)S(1)}, bf16[8,128,128]{2,1,0:T(8,128)(2,1)S(1)}, u32[]{:S(2)}, u32[]{:S(2)}) collective-permute-start(bf16[8,128,128]{2,1,0:T(8,128)(2,1)S(1)} %get-tuple-element.18), channel_id=1, source_target_pairs={{0,4},{4,0},{1,5},{5,1},{2,6},{6,2},{3,7},{7,3},{8,12},{12,8},{9,1... | collective-permute-start | bytes 786440 | tf_op jit(solution)/shard_map/ppermute | solution.py:261
  64.6 15.5 %collective-permute-start.3 = (bf16[8,128,128]{2,1,0:T(8,128)(2,1)S(1)}, bf16[8,128,128]{2,1,0:T(8,128)(2,1)S(1)}, u32[]{:S(2)}, u32[]{:S(2)}) collective-permute-start(bf16[8,128,128]{2,1,0:T(8,128)(2,1)S(1)} %get-tuple-element.16.refs_0_), channel_id=1, source_target_pairs={{0,1},{1,0},{2,3},{3,2},{4,5},{5,4},{6,7},{7,6},{8,9},{9,8},{10,11... | collective-permute-start | bytes 786440 | tf_op jit(solution)/shard_map/ppermute | solution.py:264
  64.6 17.0 %collective-permute-start = (bf16[8,128,128]{2,1,0:T(8,128)(2,1)S(1)}, bf16[8,128,128]{2,1,0:T(8,128)(2,1)}, u32[]{:S(2)}, u32[]{:S(2)}) collective-permute-start(bf16[8,128,128]{2,1,0:T(8,128)(2,1)S(1)} %get-tuple-element.16.refs_0_), channel_id=1, source_target_pairs={{0,8},{8,0},{1,9},{9,1},{2,10},{10,2},{3,11},{11,3},{4,12},{12,4},... | collective-permute-start | bytes 786440 | tf_op jit(solution)/shard_map/ppermute | solution.py:260
  79.0 1.1 copy-start.1
  80.1 0.7 copy-start.2
  80.1 0.8 copy-start.4
  80.9 0.7 copy-start.6
  81.6 4.2 %copy-start.5 = (bf16[8,128,128]{2,1,0:T(8,128)(2,1)S(1)}, bf16[8,128,128]{2,1,0:T(8,128)(2,1)}, u32[]{:S(2)}) copy-start(bf16[8,128,128]{2,1,0:T(8,128)(2,1)} %copy-done.4) | copy-start | bytes 786436
  81.6 4.5 %copy-start.3 = (bf16[8,128,128]{2,1,0:T(8,128)(2,1)S(1)}, bf16[8,128,128]{2,1,0:T(8,128)(2,1)}, u32[]{:S(2)}) copy-start(bf16[8,128,128]{2,1,0:T(8,128)(2,1)} %copy-done.2) | copy-start | bytes 786436
  81.6 6.2 %copy-start.7 = (bf16[8,128,128]{2,1,0:T(8,128)(2,1)S(1)}, bf16[8,128,128]{2,1,0:T(8,128)(2,1)}, u32[]{:S(2)}) copy-start(bf16[8,128,128]{2,1,0:T(8,128)(2,1)} %copy-done.6) | copy-start | bytes 786436
  81.6 27.5 %all-to-all-start.1 = ((bf16[16,128,384]{2,1,0:T(8,128)(2,1)}), bf16[16,128,384]{2,1,0:T(8,128)(2,1)S(1)}, u32[]{:S(2)}, u32[]{:S(2)}) async-start(bf16[16,128,384]{2,1,0:T(8,128)(2,1)} %copy-done.1), calls=%async_computation.1 | async-start | bytes 3145728 | tf_op jit(solution)/shard_map/all_to_all | solution.py:283
  85.5 1.8 %collective-permute-start.4 = (bf16[8,128,128]{2,1,0:T(8,128)(2,1)}, bf16[8,128,128]{2,1,0:T(8,128)(2,1)S(1)}, u32[]{:S(2)}, u32[]{:S(2)}) collective-permute-start(bf16[8,128,128]{2,1,0:T(8,128)(2,1)} %collective-permute-done.refs_2_), channel_id=1, source_target_pairs={{0,1},{1,0},{2,3},{3,2},{4,5},{5,4},{6,7},{7,6},{8,9},{9,8},{10,11... | collective-permute-start | bytes 786440 | tf_op jit(solution)/shard_map/ppermute | solution.py:282
  85.8 1.7 %collective-permute-start.5 = (bf16[8,128,128]{2,1,0:T(8,128)(2,1)S(1)}, bf16[8,128,128]{2,1,0:T(8,128)(2,1)S(1)}, u32[]{:S(2)}, u32[]{:S(2)}) collective-permute-start(bf16[8,128,128]{2,1,0:T(8,128)(2,1)S(1)} %copy-done.5), channel_id=1, source_target_pairs={{0,1},{1,0},{2,3},{3,2},{4,5},{5,4},{6,7},{7,6},{8,9},{9,8},{10,11... | collective-permute-start | bytes 786440 | tf_op jit(solution)/shard_map/ppermute | solution.py:282
  86.1 1.8 %collective-permute-start.6 = (bf16[8,128,128]{2,1,0:T(8,128)(2,1)S(1)}, bf16[8,128,128]{2,1,0:T(8,128)(2,1)S(1)}, u32[]{:S(2)}, u32[]{:S(2)}) collective-permute-start(bf16[8,128,128]{2,1,0:T(8,128)(2,1)S(1)} %copy-done.3), channel_id=1, source_target_pairs={{0,1},{1,0},{2,3},{3,2},{4,5},{5,4},{6,7},{7,6},{8,9},{9,8},{10,11... | collective-permute-start | bytes 786440 | tf_op jit(solution)/shard_map/ppermute | solution.py:282
  90.6 9.7 %collective-permute-start.7 = (bf16[128,1024]{1,0:T(8,128)(2,1)S(1)}, bf16[128,1024]{1,0:T(8,128)(2,1)S(1)}, u32[]{:S(2)}, u32[]{:S(2)}) collective-permute-start(bf16[128,1024]{1,0:T(8,128)(2,1)S(1)} %get-tuple-element.24), channel_id=1, source_target_pairs={{0,32},{32,64},{64,96},{96,0},{1,33},{33,65},{65,97},{97,1},{2,34}... | collective-permute-start | bytes 786440 | tf_op jit(solution)/shard_map/ppermute | solution.py:297
  92.2 14.8 %collective-permute-start.8 = (bf16[128,1024]{1,0:T(8,128)(2,1)S(1)}, bf16[128,1024]{1,0:T(8,128)(2,1)S(1)}, u32[]{:S(2)}, u32[]{:S(2)}) collective-permute-start(bf16[128,1024]{1,0:T(8,128)(2,1)S(1)} %get-tuple-element.25), channel_id=1, source_target_pairs={{0,64},{32,96},{64,0},{96,32},{1,65},{33,97},{65,1},{97,33},{2,66}... | collective-permute-start | bytes 786440 | tf_op jit(solution)/shard_map/ppermute | solution.py:297
  94.9 12.0 %collective-permute-start.9 = (bf16[128,1024]{1,0:T(8,128)(2,1)S(1)}, bf16[128,1024]{1,0:T(8,128)(2,1)S(1)}, u32[]{:S(2)}, u32[]{:S(2)}) collective-permute-start(bf16[128,1024]{1,0:T(8,128)(2,1)S(1)} %get-tuple-element.26), channel_id=1, source_target_pairs={{0,96},{32,0},{64,32},{96,64},{1,97},{33,1},{65,33},{97,65},{2,98}... | collective-permute-start | bytes 786440 | tf_op jit(solution)/shard_map/ppermute | solution.py:297
  109.1 11.3 %all-to-all-start.2 = ((bf16[8,16,1024]{2,1,0:T(8,128)(2,1)}), bf16[8,16,1024]{2,1,0:T(8,128)(2,1)S(1)}, u32[]{:S(2)}, u32[]{:S(2)}) async-start(bf16[8,16,1024]{2,1,0:T(8,128)(2,1)} %sum_tiles.1), calls=%async_computation.2 | async-start | bytes 524288 | tf_op jit(solution)/shard_map/all_to_all | solution.py:301

commit v5 on v4

--- a/solution.py
+++ b/solution.py
@@ -122,6 +122,22 @@
     )(*scalars, *arrays)
 
 
+def after_kernel(*refs):
+    pass
+
+
+def after(value, *others):
+    anywhere = pl.BlockSpec(memory_space=pl.ANY)
+    return pl.pallas_call(
+        after_kernel,
+        out_shape=jax.ShapeDtypeStruct(value.shape, value.dtype),
+        in_specs=[anywhere] * (1 + len(others)),
+        out_specs=anywhere,
+        input_output_aliases={0: 0},
+        name="after",
+    )(value, *others)
+
+
 def pack_kernel(up, w_out, queries, keys, values, packed, up_t):
     step = pl.program_id(0)
 
@@ -276,7 +292,7 @@
         ],
         flops=4_000_000_000,
     )
-    d_qkv, over_z, over_core = lax.optimization_barrier((d_qkv, over_z, over_core))
+    d_qkv = after(d_qkv, *over_z, over_core)
     parts = [near, over_core]
     for part in over_z:
         parts += [part, lax.ppermute(part, "core", flip)]

time: 122 us -> 121 us (level)
    ppermute x1, starting transfers between devices: 3.18 us -> 0.94 us  [on_device(): lax.ppermute(near, 'z1', flip)]
    ppermute x1, starting transfers between devices: 0.01 us -> 1.52 us  [on_device(): lax.ppermute(far, 'z0', flip)]
    unnamed x16 -> x12, local copies, waits for them, and re-layouts: 2.6 us -> 1.84 us
  transfers between devices with their start and end apart: 13 -> 13, of which waited for: 8 -> 8; matrix products, arithmetic and copies ran while one was open for 0% -> 0% of each run, Pallas kernels for 13% -> 14%
where the time goes in v5:
time: 121 us
  waiting for transfers between devices  59.5 us (49%)
  Pallas kernels  31.4 us (26%)
  starting transfers between devices  27.2 us (22%)
  local copies, waits for them, and re-layouts  1.84 us (2%)
    all_to_all x1, waiting for transfers between devices, on_device(): packed = lax.all_to_all(pack(rows, up, w_out), SEQ, 0, 0, tiled=True)  40.5 us
    pallas_call x6, Pallas kernels, whole_call(): pl.pallas_call(kernel, grid=(1,), out_shape=out, in_specs=[pl.BlockSpec(m...  23.8 us
    ppermute x3, waiting for transfers between devices, on_device(): lax.ppermute(tiles[far], 'x', [(i, (i + far) % 4) for i in range(4)])  10.6 us
    all_to_all x1, starting transfers between devices, on_device(): packed = lax.all_to_all(pack(rows, up, w_out), SEQ, 0, 0, tiled=True)  8.13 us
    pallas_call x1, Pallas kernels, pack(): pl.pallas_call(pack_kernel, grid=(steps,), out_shape=jax.ShapeDtypeStruct...  7.67 us
    ppermute x3, starting transfers between devices, on_device(): lax.ppermute(tiles[far], 'x', [(i, (i + far) % 4) for i in range(4)])  5.72 us
    all_to_all x1, waiting for transfers between devices, on_device(): parts = lax.all_to_all(parts, eight, 0, 0, tiled=True)  5.69 us
    all_to_all x1, starting transfers between devices, on_device(): parts = lax.all_to_all(parts, eight, 0, 0, tiled=True)  4.44 us
  transfers between devices with their start and end apart: 13, of which 8 were waited for; matrix products, arithmetic and copies ran while one was open for 0% of the time, Pallas kernels for 14%

profile of v5, /device:TPU:0, one launch (start us, length us, event | category | flops | bytes accessed | tf_op | source)
XLA Modules:
  0.0 120.8 jit_solution(16060219798410790373)
XLA Ops:
  0.6 7.7 %pack.1 = bf16[16,128,768]{2,1,0:T(8,128)(2,1)} custom-call(bf16[128,2048]{1,0:T(8,128)(2,1)} %bitcast.12, bf16[2048,2048]{1,0:T(8,128)(2,1)} %w_out.1, bf16[128,6144]{1,0:T(8,128)(2,1)} %bitcast.8, bf16[128,6144]{1,0:T(8,128)(2,1)} %bitcast.9, bf16[128,6144]{1,0:T(8,128)(2,1)} %bitcast.10), custom_call_target="tpu_custom_call" | custom-call | flops 1073741824 | bytes 8388608 | tf_op jit(solution)/shard_map/pack/pallas_call | solution.py:176
  8.3 8.1 %all-to-all-start = ((bf16[16,128,768]{2,1,0:T(8,128)(2,1)}), bf16[16,128,768]{2,1,0:T(8,128)(2,1)S(1)}, u32[]{:S(2)}, u32[]{:S(2)}) async-start(bf16[16,128,768]{2,1,0:T(8,128)(2,1)} %pack.1), calls=%async_computation | async-start | bytes 6291456 | tf_op jit(solution)/shard_map/all_to_all | solution.py:263
  16.5 0.1 pad_add_fusion.place
  16.5 40.5 %all-to-all-done.qkv.columns = bf16[16,128,768]{2,1,0:T(8,128)(2,1)S(1)} async-done(((bf16[16,128,768]{2,1,0:T(8,128)(2,1)}), bf16[16,128,768]{2,1,0:T(8,128)(2,1)S(1)}, u32[]{:S(2)}, u32[]{:S(2)}) %all-to-all-start) | async-done | bytes 3145760 | tf_op jit(solution)/shard_map/all_to_all | solution.py:263
  57.0 0.0 copy-start
  57.0 6.0 %forward.1 = (bf16[8,128,128]{2,1,0:T(8,128)(2,1)S(1)}, bf16[8,128,128]{2,1,0:T(8,128)(2,1)S(1)}, f32[16,2,128]{2,1,0:T(2,128)S(1)}) custom-call(s32[4]{0:T(128)S(1)} %pad_add_fusion.place, bf16[16,128,768]{2,1,0:T(8,128)(2,1)S(1)} %all-to-all-done.qkv.columns), custom_call_target="tpu_custom_call" | custom-call | flops 2000000000 | bytes 3686400 | tf_op jit(solution)/shard_map/forward/pallas_call | solution.py:111
  63.0 0.0 copy-start.4
  63.0 0.1 collective-permute-start
  63.1 0.9 collective-permute-start.1
  64.1 1.5 %collective-permute-start.3 = (bf16[8,128,128]{2,1,0:T(8,128)(2,1)S(1)}, bf16[8,128,128]{2,1,0:T(8,128)(2,1)}, u32[]{:S(2)}, u32[]{:S(2)}) collective-permute-start(bf16[8,128,128]{2,1,0:T(8,128)(2,1)S(1)} %get-tuple-element.12), channel_id=1, source_target_pairs={{0,4},{4,0},{1,5},{5,1},{2,6},{6,2},{3,7},{7,3},{8,12},{12,8},{9,1... | collective-permute-start | bytes 786440 | tf_op jit(solution)/shard_map/ppermute | solution.py:277
  65.6 1.7 %collective-permute-start.5 = (bf16[8,128,128]{2,1,0:T(8,128)(2,1)S(1)}, bf16[8,128,128]{2,1,0:T(8,128)(2,1)}, u32[]{:S(2)}, u32[]{:S(2)}) collective-permute-start(bf16[8,128,128]{2,1,0:T(8,128)(2,1)S(1)} %get-tuple-element.12), channel_id=1, source_target_pairs={{0,12},{4,8},{8,4},{12,0},{1,13},{5,9},{9,5},{13,1},{2,14},{6,10},... | collective-permute-start | bytes 786440 | tf_op jit(solution)/shard_map/ppermute | solution.py:278
  67.3 0.0 copy-done
  67.3 11.1 %backward.1.refs_0_ = bf16[16,128,384]{2,1,0:T(8,128)(2,1)S(1)} custom-call(bf16[16,128,768]{2,1,0:T(8,128)(2,1)S(1)} %all-to-all-done.qkv.columns, f32[16,2,128]{2,1,0:T(2,128)S(1)} %get-tuple-element.17.stats), custom_call_target="tpu_custom_call" | custom-call | flops 4000000000 | bytes 4734976 | tf_op jit(solution)/shard_map/backward/pallas_call | solution.py:111
  78.5 0.0 copy-done.4
  78.5 0.0 copy-start.1
  78.5 1.1 copy-done.1
  79.6 0.0 collective-permute-done.refs_1_.refs_4_
  79.6 0.0 copy-start.2
  79.6 0.0 collective-permute-done.1.refs_2_.refs_1_
  79.6 0.0 collective-permute-done.3.refs_4_.refs_2_
  79.6 0.0 collective-permute-done.5.refs_6_.refs_3_
  79.7 0.7 copy-done.2
  80.3 0.0 copy-start.3
  80.3 0.0 copy-start.5
  80.3 3.8 %all-to-all-start.1 = ((bf16[16,128,384]{2,1,0:T(8,128)(2,1)}), bf16[16,128,384]{2,1,0:T(8,128)(2,1)S(1)}, u32[]{:S(2)}, u32[]{:S(2)}) async-start(bf16[16,128,384]{2,1,0:T(8,128)(2,1)} %after.1), calls=%async_computation.1 | async-start | bytes 3145728 | tf_op jit(solution)/shard_map/all_to_all | solution.py:299
  84.2 0.3 collective-permute-start.2
  84.5 0.3 collective-permute-start.4
  84.8 0.2 collective-permute-start.6
  85.0 1.0 collective-permute-done.2.refs_3_
  86.0 0.4 collective-permute-done.4.refs_5_
  86.4 0.4 collective-permute-done.6.refs_7_
  86.8 0.0 copy-done.3
  86.8 0.0 copy-done.5
  86.8 3.0 %tile.1 = (bf16[128,1024]{1,0:T(8,128)(2,1)S(1)}, bf16[128,1024]{1,0:T(8,128)(2,1)S(1)}, bf16[128,1024]{1,0:T(8,128)(2,1)S(1)}, bf16[128,1024]{1,0:T(8,128)(2,1)S(1)}) custom-call(s32[4]{0:T(128)S(1)} %pad_add_fusion.place, bf16[16,128,768]{2,1,0:T(8,128)(2,1)} %copy-done, bf16[8,128,128]{2,1,0:T(8,128)(2,1)S(1)} %copy-done.5, ...), custom_call_target="tpu_custom_call" | custom-call | flops 1073741824 | bytes 6291456 | tf_op jit(solution)/shard_map/tile/pallas_call | solution.py:111
  89.7 1.6 %collective-permute-start.7 = (bf16[128,1024]{1,0:T(8,128)(2,1)S(1)}, bf16[128,1024]{1,0:T(8,128)(2,1)S(1)}, u32[]{:S(2)}, u32[]{:S(2)}) collective-permute-start(bf16[128,1024]{1,0:T(8,128)(2,1)S(1)} %get-tuple-element.14), channel_id=1, source_target_pairs={{0,32},{32,64},{64,96},{96,0},{1,33},{33,65},{65,97},{97,1},{2,34}... | collective-permute-start | bytes 786440 | tf_op jit(solution)/shard_map/ppermute | solution.py:313
  91.3 2.7 %collective-permute-start.8 = (bf16[128,1024]{1,0:T(8,128)(2,1)S(1)}, bf16[128,1024]{1,0:T(8,128)(2,1)S(1)}, u32[]{:S(2)}, u32[]{:S(2)}) collective-permute-start(bf16[128,1024]{1,0:T(8,128)(2,1)S(1)} %get-tuple-element.15), channel_id=1, source_target_pairs={{0,64},{32,96},{64,0},{96,32},{1,65},{33,97},{65,1},{97,33},{2,66}... | collective-permute-start | bytes 786440 | tf_op jit(solution)/shard_map/ppermute | solution.py:313
  94.0 1.4 %collective-permute-start.9 = (bf16[128,1024]{1,0:T(8,128)(2,1)S(1)}, bf16[128,1024]{1,0:T(8,128)(2,1)S(1)}, u32[]{:S(2)}, u32[]{:S(2)}) collective-permute-start(bf16[128,1024]{1,0:T(8,128)(2,1)S(1)} %get-tuple-element.16), channel_id=1, source_target_pairs={{0,96},{32,0},{64,32},{96,64},{1,97},{33,1},{65,33},{97,65},{2,98}... | collective-permute-start | bytes 786440 | tf_op jit(solution)/shard_map/ppermute | solution.py:313
  95.5 4.0 %collective-permute-done.7.refs_1_ = bf16[128,1024]{1,0:T(8,128)(2,1)S(1)} collective-permute-done((bf16[128,1024]{1,0:T(8,128)(2,1)S(1)}, bf16[128,1024]{1,0:T(8,128)(2,1)S(1)}, u32[]{:S(2)}, u32[]{:S(2)}) %collective-permute-start.7) | collective-permute-done | bytes 262176 | tf_op jit(solution)/shard_map/ppermute | solution.py:313
  99.4 6.6 %collective-permute-done.8.refs_2_ = bf16[128,1024]{1,0:T(8,128)(2,1)S(1)} collective-permute-done((bf16[128,1024]{1,0:T(8,128)(2,1)S(1)}, bf16[128,1024]{1,0:T(8,128)(2,1)S(1)}, u32[]{:S(2)}, u32[]{:S(2)}) %collective-permute-start.8) | collective-permute-done | bytes 262176 | tf_op jit(solution)/shard_map/ppermute | solution.py:313
  106.0 0.0 collective-permute-done.9.refs_3_
  106.0 0.8 sum_tiles.1
  106.9 1.0 all-to-all-done.1.packed
  107.8 4.4 %all-to-all-start.2 = ((bf16[8,16,1024]{2,1,0:T(8,128)(2,1)}), bf16[8,16,1024]{2,1,0:T(8,128)(2,1)S(1)}, u32[]{:S(2)}, u32[]{:S(2)}) async-start(bf16[8,16,1024]{2,1,0:T(8,128)(2,1)} %sum_tiles.1), calls=%async_computation.2 | async-start | bytes 524288 | tf_op jit(solution)/shard_map/all_to_all | solution.py:317
  112.3 1.6 %unpack_heads.1 = bf16[128,6144]{1,0:T(8,128)(2,1)} custom-call(bf16[16,128,384]{2,1,0:T(8,128)(2,1)S(1)} %all-to-all-done.1.packed), custom_call_target="tpu_custom_call" | custom-call | bytes 3145728 | tf_op jit(solution)/shard_map/unpack_heads/pallas_call | solution.py:111
  113.9 5.7 %all-to-all-done.2.parts = bf16[8,16,1024]{2,1,0:T(8,128)(2,1)S(1)} async-done(((bf16[8,16,1024]{2,1,0:T(8,128)(2,1)}), bf16[8,16,1024]{2,1,0:T(8,128)(2,1)S(1)}, u32[]{:S(2)}, u32[]{:S(2)}) %all-to-all-start.2) | async-done | bytes 262176 | tf_op jit(solution)/shard_map/all_to_all | solution.py:317
  119.6 1.2 %combine.1 = f32[16,2048]{1,0:T(8,128)} custom-call(s32[4]{0:T(128)S(1)} %pad_add_fusion.place, bf16[8,16,1024]{2,1,0:T(8,128)(2,1)S(1)} %all-to-all-done.2.parts), custom_call_target="tpu_custom_call" | custom-call | bytes 393216 | tf_op jit(solution)/shard_map/combine/pallas_call | solution.py:111
  (1 shorter events, 0.0 us)
Async XLA Ops:
  8.3 48.7 %all-to-all-start = ((bf16[16,128,768]{2,1,0:T(8,128)(2,1)}), bf16[16,128,768]{2,1,0:T(8,128)(2,1)S(1)}, u32[]{:S(2)}, u32[]{:S(2)}) async-start(bf16[16,128,768]{2,1,0:T(8,128)(2,1)} %pack.1), calls=%async_computation | async-start | bytes 6291456 | tf_op jit(solution)/shard_map/all_to_all | solution.py:263
  57.0 10.3 %copy-start = (bf16[16,128,768]{2,1,0:T(8,128)(2,1)}, bf16[16,128,768]{2,1,0:T(8,128)(2,1)S(1)}, u32[]{:S(2)}) copy-start(bf16[16,128,768]{2,1,0:T(8,128)(2,1)S(1)} %all-to-all-done.qkv.columns) | copy-start | bytes 9437188
  63.0 15.4 %copy-start.4 = (bf16[8,128,128]{2,1,0:T(8,128)(2,1)}, bf16[8,128,128]{2,1,0:T(8,128)(2,1)S(1)}, u32[]{:S(2)}) copy-start(bf16[8,128,128]{2,1,0:T(8,128)(2,1)S(1)} %get-tuple-element.11.refs_0_) | copy-start | bytes 786436
  63.0 16.6 %collective-permute-start = (bf16[8,128,128]{2,1,0:T(8,128)(2,1)S(1)}, bf16[8,128,128]{2,1,0:T(8,128)(2,1)S(1)}, u32[]{:S(2)}, u32[]{:S(2)}) collective-permute-start(bf16[8,128,128]{2,1,0:T(8,128)(2,1)S(1)} %get-tuple-element.11.refs_0_), channel_id=1, source_target_pairs={{0,1},{1,0},{2,3},{3,2},{4,5},{5,4},{6,7},{7,6},{8,9},{9,8},{10,11... | collective-permute-start | bytes 786440 | tf_op jit(solution)/shard_map/ppermute | solution.py:280
  63.1 16.5 %collective-permute-start.1 = (bf16[8,128,128]{2,1,0:T(8,128)(2,1)S(1)}, bf16[8,128,128]{2,1,0:T(8,128)(2,1)}, u32[]{:S(2)}, u32[]{:S(2)}) collective-permute-start(bf16[8,128,128]{2,1,0:T(8,128)(2,1)S(1)} %get-tuple-element.11.refs_0_), channel_id=1, source_target_pairs={{0,8},{8,0},{1,9},{9,1},{2,10},{10,2},{3,11},{11,3},{4,12},{12,4},... | collective-permute-start | bytes 786440 | tf_op jit(solution)/shard_map/ppermute | solution.py:276
  64.1 15.6 %collective-permute-start.3 = (bf16[8,128,128]{2,1,0:T(8,128)(2,1)S(1)}, bf16[8,128,128]{2,1,0:T(8,128)(2,1)}, u32[]{:S(2)}, u32[]{:S(2)}) collective-permute-start(bf16[8,128,128]{2,1,0:T(8,128)(2,1)S(1)} %get-tuple-element.12), channel_id=1, source_target_pairs={{0,4},{4,0},{1,5},{5,1},{2,6},{6,2},{3,7},{7,3},{8,12},{12,8},{9,1... | collective-permute-start | bytes 786440 | tf_op jit(solution)/shard_map/ppermute | solution.py:277
  65.6 14.1 %collective-permute-start.5 = (bf16[8,128,128]{2,1,0:T(8,128)(2,1)S(1)}, bf16[8,128,128]{2,1,0:T(8,128)(2,1)}, u32[]{:S(2)}, u32[]{:S(2)}) collective-permute-start(bf16[8,128,128]{2,1,0:T(8,128)(2,1)S(1)} %get-tuple-element.12), channel_id=1, source_target_pairs={{0,12},{4,8},{8,4},{12,0},{1,13},{5,9},{9,5},{13,1},{2,14},{6,10},... | collective-permute-start | bytes 786440 | tf_op jit(solution)/shard_map/ppermute | solution.py:278
  78.5 1.1 copy-start.1
  79.6 0.7 copy-start.2
  80.3 6.4 %copy-start.3 = (bf16[8,128,128]{2,1,0:T(8,128)(2,1)S(1)}, bf16[8,128,128]{2,1,0:T(8,128)(2,1)}, u32[]{:S(2)}) copy-start(bf16[8,128,128]{2,1,0:T(8,128)(2,1)} %copy-done.2) | copy-start | bytes 786436
  80.3 6.4 %copy-start.5 = (bf16[8,128,128]{2,1,0:T(8,128)(2,1)S(1)}, bf16[8,128,128]{2,1,0:T(8,128)(2,1)}, u32[]{:S(2)}) copy-start(bf16[8,128,128]{2,1,0:T(8,128)(2,1)} %copy-done.4) | copy-start | bytes 786436
  80.3 27.5 %all-to-all-start.1 = ((bf16[16,128,384]{2,1,0:T(8,128)(2,1)}), bf16[16,128,384]{2,1,0:T(8,128)(2,1)S(1)}, u32[]{:S(2)}, u32[]{:S(2)}) async-start(bf16[16,128,384]{2,1,0:T(8,128)(2,1)} %after.1), calls=%async_computation.1 | async-start | bytes 3145728 | tf_op jit(solution)/shard_map/all_to_all | solution.py:299
  84.2 1.8 %collective-permute-start.2 = (bf16[8,128,128]{2,1,0:T(8,128)(2,1)}, bf16[8,128,128]{2,1,0:T(8,128)(2,1)S(1)}, u32[]{:S(2)}, u32[]{:S(2)}) collective-permute-start(bf16[8,128,128]{2,1,0:T(8,128)(2,1)} %collective-permute-done.1.refs_2_.refs_1_), channel_id=1, source_target_pairs={{0,1},{1,0},{2,3},{3,2},{4,5},{5,4},{6,7},{7,6},{8,9},{9,8},{10,11... | collective-permute-start | bytes 786440 | tf_op jit(solution)/shard_map/ppermute | solution.py:298
  84.5 1.9 %collective-permute-start.4 = (bf16[8,128,128]{2,1,0:T(8,128)(2,1)}, bf16[8,128,128]{2,1,0:T(8,128)(2,1)S(1)}, u32[]{:S(2)}, u32[]{:S(2)}) collective-permute-start(bf16[8,128,128]{2,1,0:T(8,128)(2,1)} %collective-permute-done.3.refs_4_.refs_2_), channel_id=1, source_target_pairs={{0,1},{1,0},{2,3},{3,2},{4,5},{5,4},{6,7},{7,6},{8,9},{9,8},{10,11... | collective-permute-start | bytes 786440 | tf_op jit(solution)/shard_map/ppermute | solution.py:298
  84.8 2.0 %collective-permute-start.6 = (bf16[8,128,128]{2,1,0:T(8,128)(2,1)}, bf16[8,128,128]{2,1,0:T(8,128)(2,1)S(1)}, u32[]{:S(2)}, u32[]{:S(2)}) collective-permute-start(bf16[8,128,128]{2,1,0:T(8,128)(2,1)} %collective-permute-done.5.refs_6_.refs_3_), channel_id=1, source_target_pairs={{0,1},{1,0},{2,3},{3,2},{4,5},{5,4},{6,7},{7,6},{8,9},{9,8},{10,11... | collective-permute-start | bytes 786440 | tf_op jit(solution)/shard_map/ppermute | solution.py:298
  89.7 9.7 %collective-permute-start.7 = (bf16[128,1024]{1,0:T(8,128)(2,1)S(1)}, bf16[128,1024]{1,0:T(8,128)(2,1)S(1)}, u32[]{:S(2)}, u32[]{:S(2)}) collective-permute-start(bf16[128,1024]{1,0:T(8,128)(2,1)S(1)} %get-tuple-element.14), channel_id=1, source_target_pairs={{0,32},{32,64},{64,96},{96,0},{1,33},{33,65},{65,97},{97,1},{2,34}... | collective-permute-start | bytes 786440 | tf_op jit(solution)/shard_map/ppermute | solution.py:313
  91.3 14.7 %collective-permute-start.8 = (bf16[128,1024]{1,0:T(8,128)(2,1)S(1)}, bf16[128,1024]{1,0:T(8,128)(2,1)S(1)}, u32[]{:S(2)}, u32[]{:S(2)}) collective-permute-start(bf16[128,1024]{1,0:T(8,128)(2,1)S(1)} %get-tuple-element.15), channel_id=1, source_target_pairs={{0,64},{32,96},{64,0},{96,32},{1,65},{33,97},{65,1},{97,33},{2,66}... | collective-permute-start | bytes 786440 | tf_op jit(solution)/shard_map/ppermute | solution.py:313
  94.0 12.0 %collective-permute-start.9 = (bf16[128,1024]{1,0:T(8,128)(2,1)S(1)}, bf16[128,1024]{1,0:T(8,128)(2,1)S(1)}, u32[]{:S(2)}, u32[]{:S(2)}) collective-permute-start(bf16[128,1024]{1,0:T(8,128)(2,1)S(1)} %get-tuple-element.16), channel_id=1, source_target_pairs={{0,96},{32,0},{64,32},{96,64},{1,97},{33,1},{65,33},{97,65},{2,98}... | collective-permute-start | bytes 786440 | tf_op jit(solution)/shard_map/ppermute | solution.py:313
  107.8 11.7 %all-to-all-start.2 = ((bf16[8,16,1024]{2,1,0:T(8,128)(2,1)}), bf16[8,16,1024]{2,1,0:T(8,128)(2,1)S(1)}, u32[]{:S(2)}, u32[]{:S(2)}) async-start(bf16[8,16,1024]{2,1,0:T(8,128)(2,1)} %sum_tiles.1), calls=%async_computation.2 | async-start | bytes 524288 | tf_op jit(solution)/shard_map/all_to_all | solution.py:317
